TPU v7x, 32 devices: a whole 2x2x4 slice. The times are simulated.
32 devices in a mesh: groups: 2 (over y), dp: 4 (over z), tensor: 2 (over x), sub: 2 (over core).
Axes of the slice: x: 2, y: 2, z: 4, core: 2. Of those that a mesh axis runs over, the one named last changes fastest.
Arguments:
- hidden: bfloat16 [128, 32, 5120], P(('groups', 'dp'), None, ('tensor', 'sub')), parts along dimension 0, may hold values from -150 to 150
- seq_len: int32 [128], P(('groups', 'dp')), parts along dimension 0, may hold values from 1 to 32, as said below
- target_rank: int32 [128], P(('groups', 'dp')), parts along dimension 0, may hold values from 0 to 3, as said below
- in_gain: float32 [5120], replicated, may hold values from 0.25 to 1.75
- joined_projection_weight: bfloat16 [5120, 4, 1280], P('dp', 'tensor'), may hold values from -0.078125 to 0.078125
- query_gain: float32 [128], replicated, may hold values from 0.1 to 1.9
- k_gain: float32 [128], replicated, may hold values from 0.1 to 1.9
Outputs:
- key_cache: bfloat16 [128, 32, 512], P(('groups', 'dp'), 'sub', 'tensor'), parts along dimension 0
- value_cache: bfloat16 [128, 32, 512], P(('groups', 'dp'), 'sub', 'tensor'), parts along dimension 0
- context: bfloat16 [128, 32, 4, 1024], P(('groups', 'dp'), None, 'tensor', 'sub'), parts along dimension 0
There are 2 independent parts, one for each index of `groups`. A program takes and returns all parts, laid end to end along the dimension named above; an argument that names none is the same for every part. Nothing has to cross between parts.
Inputs may be any that keep to these rules, and one draw needn't show every extreme that they name: `seq_len`: positions from a sequence's length on hold padding. `target_rank`: every dp rank receives exactly 16 sequences, at most 4 of them from any one dp rank.
All inputs are finite; a program needn't handle non-finite values.
Results may differ from a plain program's by a relative error of at most 0.0075.
Values may be sent and summed in bfloat16 or wider, within the bound.
A program may use at most 128 MiB of HBM per device.

v0:
```python
import jax
import jax.numpy as jnp
from jax import lax
from jax.sharding import PartitionSpec as P

EPS = 1e-06
THETA = 1000000.0


def per_head_norm(value_rows, gain):
    square_mean = jnp.mean(value_rows * value_rows, axis=-1, keepdims=True)
    return value_rows * lax.rsqrt(square_mean + EPS) * gain


def rotary_embed(value_rows, token_positions):
    half_width = value_rows.shape[-1] // 2
    frequency = THETA ** (-(2.0 * jnp.arange(half_width, dtype=jnp.float32)) / value_rows.shape[-1])
    angle = token_positions.astype(jnp.float32)[:, None] * frequency[None, :]
    cosine = jnp.cos(angle)[None, :, None, :]
    sine = jnp.sin(angle)[None, :, None, :]
    first = value_rows[..., :half_width]
    second = value_rows[..., half_width:]
    return jnp.concatenate(
        [first * cosine - second * sine, second * cosine + first * sine], axis=-1
    )


def body(hidden, seq_len, target_rank, in_gain, joined_projection_weight, query_gain, k_gain):
    slots, length, width = hidden.shape
    ranks = lax.axis_size("dp")
    pair = -(-slots // ranks)
    lanes = ranks * pair
    local = jnp.arange(slots, dtype=jnp.int32)
    same_target = (target_rank[:, None] == target_rank[None, :]) & (local[None, :] < local[:, None])
    earlier = jnp.sum(same_target.astype(jnp.int32), axis=1)
    position = target_rank * pair + earlier
    lane_ids = jnp.arange(lanes, dtype=jnp.int32)
    hits = lane_ids[:, None] == position[None, :]
    filled = jnp.any(hits, axis=1)
    source = jnp.sum(jnp.where(hits, local[None, :], 0), axis=1)
    outgoing = jnp.where(
        filled[:, None, None], jnp.take(hidden, source, axis=0), jnp.zeros((), hidden.dtype)
    )
    sent_length = jnp.where(filled, jnp.take(seq_len, source), 0)
    arrived, arrived_length = (
        lax.all_to_all(
            outgoing.reshape(ranks, pair, length, width),
            "dp",
            split_axis=0,
            concat_axis=0,
            tiled=True,
        ),
        lax.all_to_all(
            sent_length.reshape(ranks, pair), "dp", split_axis=0, concat_axis=0, tiled=True
        ),
    )
    arrived = arrived.reshape(lanes, length, width)
    arrived_length = arrived_length.reshape(lanes)
    present = arrived_length > 0
    arrived_slot = jnp.cumsum(present.astype(jnp.int32)) - 1
    matches = (arrived_slot[None, :] == local[:, None]) & present[None, :]
    chosen = jnp.sum(jnp.where(matches, lane_ids[None, :], 0), axis=1)
    lengths = jnp.sum(jnp.where(matches, arrived_length[None, :], 0), axis=1)
    moved = jnp.take(arrived, chosen, axis=0)
    whole = lax.all_gather(moved, ("tensor", "sub"), axis=2, tiled=True)
    tokens = whole.reshape(slots * length, whole.shape[2]).astype(jnp.float32)
    square_mean = jnp.mean(tokens * tokens, axis=-1, keepdims=True)
    normed_query = (tokens * lax.rsqrt(square_mean + EPS) * in_gain).astype(jnp.bfloat16)
    groups = joined_projection_weight.shape[1]
    head_dim = query_gain.shape[0]
    group_query = joined_projection_weight.shape[2] - 2 * head_dim
    half_heads = group_query // head_dim // lax.axis_size("sub")
    query_cols = half_heads * head_dim
    core = lax.axis_index("sub")
    own_query = lax.dynamic_slice_in_dim(joined_projection_weight, core * query_cols, query_cols, 2)
    extra = joined_projection_weight[:, :, group_query:]
    columns = jnp.concatenate([own_query, extra], axis=2)
    span = columns.shape[2]
    flat_columns = columns.reshape(columns.shape[0], groups * span)
    mixed_projection = jnp.dot(
        normed_query,
        lax.all_gather(flat_columns, "dp", axis=0, tiled=True),
        preferred_element_type=jnp.float32,
    )
    mixed_projection = mixed_projection.reshape(slots, length, groups, span)
    token_positions = jnp.arange(length, dtype=jnp.int32)
    live = token_positions[None, :] < lengths[:, None]
    query_rows = mixed_projection[..., :query_cols].reshape(
        slots, length, groups * half_heads, head_dim
    )
    query_rows = rotary_embed(per_head_norm(query_rows, query_gain), token_positions).astype(
        jnp.bfloat16
    )
    key_rows = rotary_embed(
        per_head_norm(mixed_projection[..., query_cols : query_cols + head_dim], k_gain),
        token_positions,
    )
    key_rows = jnp.where(live[:, :, None, None], key_rows, 0.0).astype(jnp.bfloat16)
    value_rows = jnp.where(
        live[:, :, None, None], mixed_projection[..., query_cols + head_dim :], 0.0
    ).astype(jnp.bfloat16)
    grouped_heads = query_rows.reshape(slots, length, groups, half_heads, head_dim)
    scores = jnp.einsum(
        "nqghd,nkgd->nghqk", grouped_heads, key_rows, preferred_element_type=jnp.float32
    ) * head_dim ** (-0.5)
    causal = token_positions[None, :] <= token_positions[:, None]
    allowed = causal[None, None, None, :, :] & live[:, None, None, None, :]
    weights = jnp.where(allowed, jnp.exp(scores), 0.0)
    probs = (weights / jnp.sum(weights, axis=-1, keepdims=True)).astype(jnp.bfloat16)
    context = jnp.einsum("nghqk,nkgd->nqghd", probs, value_rows, preferred_element_type=jnp.float32)
    context = jnp.where(live[:, :, None, None, None], context, 0.0)
    context = context.reshape(slots, length, groups, half_heads * head_dim).astype(jnp.bfloat16)
    share = length // lax.axis_size("sub")
    key_share = lax.dynamic_slice_in_dim(key_rows, core * share, share, 1).reshape(
        slots, share, groups * head_dim
    )
    value_share = lax.dynamic_slice_in_dim(value_rows, core * share, share, 1).reshape(
        slots, share, groups * head_dim
    )
    return (key_share, value_share, context)


def solution(mesh):
    placed = (
        P(("groups", "dp"), None, ("tensor", "sub")),
        P(("groups", "dp")),
        P(("groups", "dp")),
        P(),
        P("dp", "tensor", None),
        P(),
        P(),
    )
    return jax.shard_map(
        body,
        mesh=mesh,
        in_specs=placed,
        out_specs=(
            P(("groups", "dp"), "sub", "tensor"),
            P(("groups", "dp"), "sub", "tensor"),
            P(("groups", "dp"), None, "tensor", "sub"),
        ),
        check_vma=False,
    )
```

profile of v0, /device:TPU:0, one launch (start us, length us, event | category | flops | bytes accessed | tf_op | source)
XLA Modules:
  0.0 408.2 jit_solution(16002357431540863237)
XLA Ops:
  7.2 1.0 convert_reduce_fusion
  8.1 0.7 multiply_add_fusion.1
  8.8 0.1 select_reduce_fusion.2
  8.9 0.1 fusion.19
  9.1 0.1 reduce_or.12
  9.2 1.3 gather_fusion
  10.6 0.6 select_select_fusion.1
  11.2 6.3 %all-to-all-start = ((s32[4,1,4]{2,1,0:T(1,128)}), s32[4,1,4]{2,1,0:T(1,128)S(1)}, u32[]{:S(2)}, u32[]{:S(2)}) async-start(s32[4,1,4]{2,1,0:T(1,128)} %bitcast.2), calls=%async_computation | async-start | bytes 4096 | tf_op jit(solution)/shard_map/all_to_all | solution.py:53
  17.6 0.6 gather_fusion.1
  18.2 4.8 %all-to-all-done = s32[4,1,4]{2,1,0:T(1,128)S(1)} async-done(((s32[4,1,4]{2,1,0:T(1,128)}), s32[4,1,4]{2,1,0:T(1,128)S(1)}, u32[]{:S(2)}, u32[]{:S(2)}) %all-to-all-start) | async-done | bytes 96 | tf_op jit(solution)/shard_map/all_to_all | solution.py:53
  23.0 0.5 broadcast.333
  23.5 0.7 reduce.6
  24.2 0.1 reshape.355
  24.3 1.3 select_select_fusion
  25.6 3.5 all-to-all-start.1
  29.3 0.1 add_reduce_fusion
  29.4 0.1 select_reduce_fusion.1
  29.6 29.7 %all-to-all-done.1 = bf16[4,4,32,1280]{3,2,1,0:T(8,128)(2,1)S(1)} async-done(((bf16[4,4,32,1280]{3,2,1,0:T(8,128)(2,1)}), bf16[4,4,32,1280]{3,2,1,0:T(8,128)(2,1)S(1)}, u32[]{:S(2)}, u32[]{:S(2)}) %all-to-all-start.1) | async-done | bytes 1310752 | tf_op jit(solution)/shard_map/all_to_all | solution.py:46
  59.3 0.6 gather_fusion.2
  59.9 1.3 broadcast_select_fusion
  61.4 4.4 %constant_dynamic-slice_fusion = bf16[1280,2,512]{2,1,0:T(2,128)(2,1)S(1)} fusion(bf16[1280,2,1280]{2,1,0:T(2,128)(2,1)} %param.13, s32[]{:T(128)S(6)} %select_n.99), kind=kLoop, calls=%fused_computation.73 | loop fusion | bytes 5242884 | tf_op jit(solution)/shard_map/dynamic_slice | solution.py:75
  65.7 5.4 %pad_maximum_fusion = bf16[1280,2,768]{2,1,0:T(2,128)(2,1)} fusion(bf16[1280,2,256]{2,1,0:T(2,128)(2,1)S(1)} %slice-done, bf16[1280,2,512]{2,1,0:T(2,128)(2,1)S(1)} %constant_dynamic-slice_fusion), kind=kLoop, calls=%fused_computation.12 | loop fusion | flops 7864320 | bytes 7864320 | tf_op jit(solution)/shard_map/concatenate | solution.py:77
  71.2 10.7 %copy.51 = bf16[1280,2,768]{0,2,1:T(8,128)(2,1)} copy(bf16[1280,2,768]{2,1,0:T(2,128)(2,1)} %pad_maximum_fusion) | data formatting | bytes 7864320 | tf_op jit(solution)/shard_map/reshape | solution.py:79
  81.9 0.1 multiply_cosine_fusion
  82.1 0.1 broadcast_and_fusion
  82.3 18.7 %all-gather.3.cloned.1.call-done = bf16[16,32,5120]{2,1,0:T(8,128)(2,1)} async-done(((bf16[16,32,1280]{2,1,0:T(8,128)(2,1)}), bf16[16,32,5120]{2,1,0:T(8,128)(2,1)}) %all-gather.3.cloned.1.call-update) | async-done | bytes 5242896 | tf_op jit(solution)/shard_map/all_gather | solution.py:65
  101.0 3.6 fusion
  104.6 267.7 %all-gather.5.cloned.1.call-done = bf16[5120,1536]{0,1:T(8,128)(2,1)} async-done(((bf16[1280,1536]{0,1:T(8,128)(2,1)}), bf16[5120,1536]{0,1:T(8,128)(2,1)}) %all-gather.5.cloned.1.call-update) | async-done | bytes 15728656 | tf_op jit(solution)/shard_map/all_gather | solution.py:82
  372.3 12.8 %fusion.4 = f32[16,32,2,768]{3,1,2,0:T(8,128)S(1)} fusion(bf16[2,768,5120,1]{2,1,0,3:T(8,128)(2,1)} %bitcast.60, bf16[16,32,5120]{2,1,0:T(8,128)(2,1)} %all-gather.3.cloned.1.call-done, f32[5120]{0:T(1024)S(1)} %copy-done.6, f32[16,32]{1,0:T(8,128)S(1)} %add_rsqrt_fusion.2), kind=kOutput, calls=%fused_computation.9 | convolution fusion | flops 8063549440 | bytes 24139776 | tf_op jit(solution)/shard_map/dot_general | solution.py:80
  385.1 0.2 multiply_reduce_fusion.1
  385.3 0.3 slice.42
  385.6 0.4 copy-done.4
  386.0 0.2 multiply_multiply_fusion.1
  386.2 0.3 multiply_subtract_fusion
  386.5 0.2 fusion.15
  386.7 0.7 copy_bitcast_fusion.1
  387.4 0.7 copy_bitcast_fusion
  388.1 3.0 copy.41
  391.1 2.9 reshape.361
  394.1 0.6 multiply_reduce_fusion
  394.7 0.9 multiply_multiply_fusion
  395.6 0.8 subtract_convert_fusion
  396.4 0.2 copy.43
  396.7 0.2 copy.42
  397.0 1.9 fusion.8
  398.9 0.8 fusion.9
  399.6 0.5 copy.52
  400.2 1.2 reshape.398
  (39 shorter events, 0.7 us)
Async XLA Ops:
  7.2 10.4 %copy-start = (bf16[16,32,1280]{2,1,0:T(8,128)(2,1)S(1)}, bf16[16,32,1280]{2,1,0:T(8,128)(2,1)}, u32[]{:S(2)}) copy-start(bf16[16,32,1280]{2,1,0:T(8,128)(2,1)} %param.9) | copy-start | bytes 3932164
  11.2 11.8 %all-to-all-start = ((s32[4,1,4]{2,1,0:T(1,128)}), s32[4,1,4]{2,1,0:T(1,128)S(1)}, u32[]{:S(2)}, u32[]{:S(2)}) async-start(s32[4,1,4]{2,1,0:T(1,128)} %bitcast.2), calls=%async_computation | async-start | bytes 4096 | tf_op jit(solution)/shard_map/all_to_all | solution.py:53
  25.6 33.7 %all-to-all-start.1 = ((bf16[4,4,32,1280]{3,2,1,0:T(8,128)(2,1)}), bf16[4,4,32,1280]{3,2,1,0:T(8,128)(2,1)S(1)}, u32[]{:S(2)}, u32[]{:S(2)}) async-start(bf16[4,4,32,1280]{3,2,1,0:T(8,128)(2,1)} %bitcast.4), calls=%async_computation.1 | async-start | bytes 2621440 | tf_op jit(solution)/shard_map/all_to_all | solution.py:46
  29.1 71.9 %all-gather.3.cloned.1.call-start = ((), (), s32[]{:S(2)}) async-start(), calls=%async_computation.2 | async-start | bytes 6553600 | tf_op jit(solution)/shard_map/all_gather | solution.py:65
  61.3 310.9 %all-gather.5.cloned.1.call-start = ((), (), s32[]{:S(2)}) async-start(), calls=%async_computation.3 | async-start | bytes 19660800 | tf_op jit(solution)/shard_map/all_gather | solution.py:82
  61.4 4.4 %slice-start = ((bf16[1280,2,1280]{2,1,0:T(2,128)(2,1)}), bf16[1280,2,256]{2,1,0:T(2,128)(2,1)S(1)}, s32[]{:S(2)}) async-start(bf16[1280,2,1280]{2,1,0:T(2,128)(2,1)} %param.13), calls=%async_computation.4 | async-start | bytes 2621440 | tf_op jit(solution)/shard_map/slice | solution.py:76
  82.3 290.0 %copy-start.6 = (f32[5120]{0:T(1024)S(1)}, f32[5120]{0:T(1024)}, u32[]{:S(2)}) copy-start(f32[5120]{0:T(1024)} %param.12) | copy-start | bytes 61444
  385.3 0.7 copy-start.4
  386.7 4.4 %copy-start.2 = (bf16[16,32,2,128]{3,1,2,0:T(8,128)(2,1)}, bf16[16,32,2,128]{3,1,2,0:T(8,128)(2,1)S(1)}, u32[]{:S(2)}) copy-start(bf16[16,32,2,128]{3,1,2,0:T(8,128)(2,1)S(1)} %get-tuple-element.19) | copy-start | bytes 786436
  394.0 0.7 copy-start.5
  396.9 1.9 copy-start.3
  398.8 2.6 copy-start.1
Sparse Core Ops, SparseCore 0:
  61.4 39.5 all-gather.2
  102.6 269.6 all-gather.4
where the time goes:
time: 409 us; the launch traced here: 408 us
  waiting for transfers between devices  321 us (78%)
  local copies, waits for them, and re-layouts  28.7 us (7%)
  other arithmetic  18.8 us (5%)
  matrix products  15.5 us (4%)
  between operations  14.4 us (4%)
  starting transfers between devices  9.94 us (2%)
    all_gather x1, waiting for transfers between devices, body(): lax.all_gather(flat_columns, 'dp', axis=0, tiled=True)  268 us
    all_to_all x1, waiting for transfers between devices, body(): lax.all_to_all(outgoing.reshape(ranks, pair, length, width), 'dp', split_...  29.7 us
    all_gather x1, waiting for transfers between devices, body(): whole = lax.all_gather(moved, ('tensor', 'sub'), axis=2, tiled=True)  18.7 us
    dot_general x1, matrix products, body(): jnp.dot(normed_query, lax.all_gather(flat_columns, 'dp', axis=0, tiled=Tr...  12.8 us
    reshape x1, local copies, waits for them, and re-layouts, body(): flat_columns = columns.reshape(columns.shape[0], groups * span)  10.7 us
  transfers between devices with their start and end apart: 4, of which 4 were waited for; matrix products, arithmetic and copies ran while one was open for 6% of the time, Pallas kernels for 0%

commit v1 on v0

--- a/solution.py
+++ b/solution.py
@@ -61,7 +61,7 @@
     matches = (arrived_slot[None, :] == local[:, None]) & present[None, :]
     chosen = jnp.sum(jnp.where(matches, lane_ids[None, :], 0), axis=1)
     lengths = jnp.sum(jnp.where(matches, arrived_length[None, :], 0), axis=1)
-    moved = jnp.take(arrived, chosen, axis=0)
+    moved = arrived if lanes == slots else jnp.take(arrived, chosen, axis=0)
     whole = lax.all_gather(moved, ("tensor", "sub"), axis=2, tiled=True)
     tokens = whole.reshape(slots * length, whole.shape[2]).astype(jnp.float32)
     square_mean = jnp.mean(tokens * tokens, axis=-1, keepdims=True)
@@ -77,9 +77,12 @@
     columns = jnp.concatenate([own_query, extra], axis=2)
     span = columns.shape[2]
     flat_columns = columns.reshape(columns.shape[0], groups * span)
+    copies = lax.axis_size("groups")
+    rows = flat_columns.shape[0] // copies
+    own_rows = lax.dynamic_slice_in_dim(flat_columns, lax.axis_index("groups") * rows, rows, 0)
     mixed_projection = jnp.dot(
         normed_query,
-        lax.all_gather(flat_columns, "dp", axis=0, tiled=True),
+        lax.all_gather(own_rows, ("dp", "groups"), axis=0, tiled=True),
         preferred_element_type=jnp.float32,
     )
     mixed_projection = mixed_projection.reshape(slots, length, groups, span)

time: 409 us -> 344 us (0.84)
  waiting for transfers between devices: 321 us -> 223 us
  blocking collectives: 0 us -> 37.6 us
  starting transfers between devices: 9.94 us -> 3.3 us
    all_gather x1, waiting for transfers between devices: 268 us -> 213 us  [body(): lax.all_gather(own_rows, ('dp', 'groups'), axis=0, tiled=True)]
    all_to_all x0 -> x1, blocking collectives: none -> 37.6 us  [body(): lax.all_to_all(outgoing.reshape(ranks, pair, length, width), 'dp', split_...]
    all_to_all x1 -> x0, waiting for transfers between devices: 29.7 us -> none  [body(): lax.all_to_all(outgoing.reshape(ranks, pair, length, width), 'dp', split_...]
    all_gather x1, waiting for transfers between devices: 18.7 us -> 4.2 us  [body(): whole = lax.all_gather(moved, ('tensor', 'sub'), axis=2, tiled=True)]
  transfers between devices with their start and end apart: 4 -> 3, of which waited for: 4 -> 3; matrix products, arithmetic and copies ran while one was open for 6% -> 9% of each run, Pallas kernels for 0% -> 0%
where the time goes in v1:
time: 344 us; the launch traced here: 343 us
  waiting for transfers between devices  223 us (65%)
  blocking collectives  37.6 us (11%)
  local copies, waits for them, and re-layouts  31.3 us (9%)
  other arithmetic  18.4 us (5%)
  matrix products  15.5 us (5%)
  between operations  14.3 us (4%)
    all_gather x1, waiting for transfers between devices, body(): lax.all_gather(own_rows, ('dp', 'groups'), axis=0, tiled=True)  213 us
    all_to_all x1, blocking collectives, body(): lax.all_to_all(outgoing.reshape(ranks, pair, length, width), 'dp', split_...  37.6 us
    dot_general x1, matrix products, body(): jnp.dot(normed_query, lax.all_gather(own_rows, ('dp', 'groups'), axis=0,...  12.8 us
    reshape x1, local copies, waits for them, and re-layouts, body(): flat_columns = columns.reshape(columns.shape[0], groups * span)  10.6 us
  transfers between devices with their start and end apart: 3, of which 3 were waited for; matrix products, arithmetic and copies ran while one was open for 9% of the time, Pallas kernels for 0%

profile of v1, /device:TPU:0, one launch (start us, length us, event | category | flops | bytes accessed | tf_op | source)
XLA Modules:
  0.0 343.4 jit_solution(11517539133538956188)
XLA Ops:
  7.2 0.9 convert_reduce_fusion
  8.2 0.7 multiply_add_fusion.1
  8.8 0.1 select_reduce_fusion.1
  9.0 0.1 fusion.19
  9.2 0.1 broadcast_in_dim.122
  9.3 0.6 gather_fusion.1
  9.9 0.3 select_select_fusion
  10.2 37.6 %all_to_all.11 = bf16[4,4,32,1280]{3,2,1,0:T(8,128)(2,1)} all-to-all(bf16[4,4,32,1280]{3,2,1,0:T(8,128)(2,1)S(1)} %select_select_fusion), channel_id=1, replica_groups=mesh['groups'=2,'dp'=4,'tensor'=2,'sub'=2] {'dp'}, dimensions={0} | all-to-all | bytes 2621440 | tf_op jit(solution)/shard_map/all_to_all | solution.py:46
  47.8 4.4 %constant_dynamic-slice_fusion.1 = bf16[1280,2,512]{2,1,0:T(2,128)(2,1)S(1)} fusion(bf16[1280,2,1280]{2,1,0:T(2,128)(2,1)} %param.11, s32[]{:T(128)S(6)} %select_n.105), kind=kLoop, calls=%fused_computation.67 | loop fusion | bytes 5242884 | tf_op jit(solution)/shard_map/dynamic_slice | solution.py:75
  52.2 5.4 %pad_maximum_fusion = bf16[1280,2,768]{2,1,0:T(2,128)(2,1)} fusion(bf16[1280,2,256]{2,1,0:T(2,128)(2,1)S(1)} %slice-done, bf16[1280,2,512]{2,1,0:T(2,128)(2,1)S(1)} %constant_dynamic-slice_fusion.1), kind=kLoop, calls=%fused_computation.11 | loop fusion | flops 7864320 | bytes 7864320 | tf_op jit(solution)/shard_map/concatenate | solution.py:77
  57.6 10.6 %copy.51 = bf16[1280,2,768]{0,2,1:T(8,128)(2,1)} copy(bf16[1280,2,768]{2,1,0:T(2,128)(2,1)} %pad_maximum_fusion) | data formatting | bytes 7864320 | tf_op jit(solution)/shard_map/reshape | solution.py:79
  68.2 3.0 constant_dynamic-slice_fusion
  71.3 0.1 reduce_or.12
  71.4 0.7 gather_fusion
  72.1 0.1 gather.13
  72.2 0.6 select_select_fusion.1
  72.8 3.2 all-to-all-start
  76.0 0.1 multiply_cosine_fusion
  76.2 5.3 %all-to-all-done = s32[4,1,4]{2,1,0:T(1,128)S(1)} async-done(((s32[4,1,4]{2,1,0:T(1,128)}), s32[4,1,4]{2,1,0:T(1,128)S(1)}, u32[]{:S(2)}, u32[]{:S(2)}) %all-to-all-start) | async-done | bytes 96 | tf_op jit(solution)/shard_map/all_to_all | solution.py:53
  81.4 0.5 broadcast.312
  81.9 0.7 reduce.6
  82.6 0.1 reshape.353
  82.8 0.1 add_reduce_fusion
  82.9 0.1 select_reduce_fusion
  83.1 0.1 broadcast_and_fusion
  83.3 4.2 %all-gather.3.cloned.1.call-done = bf16[16,32,5120]{2,1,0:T(8,128)(2,1)} async-done(((bf16[16,32,1280]{2,1,0:T(8,128)(2,1)}), bf16[16,32,5120]{2,1,0:T(8,128)(2,1)}) %all-gather.3.cloned.1.call-update) | async-done | bytes 5242896 | tf_op jit(solution)/shard_map/all_gather | solution.py:65
  87.5 3.6 %fusion = f32[16,32]{1,0:T(8,128)S(1)} fusion(bf16[16,32,5120]{2,1,0:T(8,128)(2,1)} %all-gather.3.cloned.1.call-done), kind=kLoop, calls=%fused_computation.4 | loop fusion | flops 7863808 | bytes 5244928 | tf_op jit(solution)/shard_map/reduce_sum | solution.py:67
  91.1 213.5 %all-gather.5.cloned.1.call-done = bf16[5120,1536]{0,1:T(8,128)(2,1)} async-done(((bf16[640,1536]{0,1:T(8,128)(2,1)}), bf16[5120,1536]{0,1:T(8,128)(2,1)}) %all-gather.5.cloned.1.call-update) | async-done | bytes 15728656 | tf_op jit(solution)/shard_map/all_gather | solution.py:85
  304.6 12.8 %fusion.4 = f32[16,32,2,768]{3,1,2,0:T(8,128)S(1)} fusion(bf16[2,768,5120,1]{2,1,0,3:T(8,128)(2,1)} %bitcast.63, bf16[16,32,5120]{2,1,0:T(8,128)(2,1)} %all-gather.3.cloned.1.call-done, f32[5120]{0:T(1024)S(1)} %copy-done.6, f32[16,32]{1,0:T(8,128)S(1)} %add_rsqrt_fusion.2), kind=kOutput, calls=%fused_computation.8 | convolution fusion | flops 8063549440 | bytes 24139776 | tf_op jit(solution)/shard_map/dot_general | solution.py:83
  317.4 0.2 multiply_reduce_fusion.1
  317.7 0.3 slice.40
  317.9 1.2 copy-done.3
  319.1 3.0 copy.41
  322.1 2.9 reshape.358
  325.1 0.6 multiply_reduce_fusion
  325.8 1.2 multiply_multiply_fusion.1
  327.0 0.9 multiply_multiply_fusion
  327.9 0.2 multiply_subtract_fusion
  328.2 0.8 subtract_convert_fusion
  329.0 0.2 copy.42
  329.2 0.2 copy.43
  329.5 1.3 fusion.15
  330.8 1.9 fusion.8
  332.6 0.8 fusion.9
  333.4 0.5 copy.52
  334.0 1.2 reshape.381
  335.2 0.7 copy.58
  335.9 0.7 copy.59
  (36 shorter events, 0.7 us)
Async XLA Ops:
  7.2 2.1 copy-start
  7.2 80.3 %all-gather.3.cloned.1.call-start = ((), (), s32[]{:S(2)}) async-start(), calls=%async_computation.2 | async-start | bytes 6553600 | tf_op jit(solution)/shard_map/all_gather | solution.py:65
  47.8 256.8 %all-gather.5.cloned.1.call-start = ((), (), s32[]{:S(2)}) async-start(), calls=%async_computation.3 | async-start | bytes 17694720 | tf_op jit(solution)/shard_map/all_gather | solution.py:85
  47.8 4.4 %slice-start = ((bf16[1280,2,1280]{2,1,0:T(2,128)(2,1)}), bf16[1280,2,256]{2,1,0:T(2,128)(2,1)S(1)}, s32[]{:S(2)}) async-start(bf16[1280,2,1280]{2,1,0:T(2,128)(2,1)} %param.11), calls=%async_computation.4 | async-start | bytes 2621440 | tf_op jit(solution)/shard_map/slice | solution.py:76
  68.2 3.2 copy-start.2
  72.8 8.7 %all-to-all-start = ((s32[4,1,4]{2,1,0:T(1,128)}), s32[4,1,4]{2,1,0:T(1,128)S(1)}, u32[]{:S(2)}, u32[]{:S(2)}) async-start(s32[4,1,4]{2,1,0:T(1,128)} %bitcast.2), calls=%async_computation | async-start | bytes 4096 | tf_op jit(solution)/shard_map/all_to_all | solution.py:53
  83.3 221.3 %copy-start.6 = (f32[5120]{0:T(1024)S(1)}, f32[5120]{0:T(1024)}, u32[]{:S(2)}) copy-start(f32[5120]{0:T(1024)} %param.10) | copy-start | bytes 61444
  317.4 1.7 copy-start.3
  325.1 0.7 copy-start.4
  325.1 1.9 copy-start.5
  333.4 3.2 copy-start.1
Sparse Core Ops, SparseCore 0:
  47.9 39.5 all-gather.2
  89.7 214.8 all-gather.4

commit v2 on v1

--- a/solution.py
+++ b/solution.py
@@ -1,6 +1,10 @@
+import functools
+
 import jax
 import jax.numpy as jnp
 from jax import lax
+from jax.experimental import pallas as pl
+from jax.experimental.pallas import tpu as pltpu
 from jax.sharding import PartitionSpec as P
 
 EPS = 1e-06
@@ -123,7 +127,416 @@
     return (key_share, value_share, context)
 
 
+CHUNK = 256
+
+
+def exchange_kernel(
+    tok, lens, w, q_out, kv_out, len_out,
+    a, wm, psend, prec, own, ssend, srecv, kvown, kvrecv, lrecv,
+    s1s, s1r, s2s, s2r, s3s, s3r, s4s, s4r,
+    ws, wr, wfs, wfr, ps, pr, ss, sr, ls, lr, kvs, kvr,
+):
+    g = lax.axis_index("groups")
+    z = lax.axis_index("dp")
+    x = lax.axis_index("tensor")
+    s = lax.axis_index("sub")
+    here = z % 2
+    pair = z // 2
+    half = w.shape[1] // 2
+    n_chunks = w.shape[0]
+    x_mate = (g, z, 1 - x, s)
+    sibling = (g, z, x, 1 - s)
+    z_mate = (g, pair * 2 + (1 - here), x, s)
+    y_mate = (1 - g, z, x, s)
+    far = (g, (1 - pair) * 2 + here, x, s)
+
+    barrier = pltpu.get_barrier_semaphore()
+    for dz in range(1, 4):
+        for dx in range(2):
+            pl.semaphore_signal(
+                barrier, inc=1, device_id=(g, (z + dz) % 4, (x + dx) % 2, s),
+                device_id_type=pl.DeviceIdType.MESH,
+            )
+    for other in (x_mate, sibling, y_mate):
+        pl.semaphore_signal(barrier, inc=1, device_id=other, device_id_type=pl.DeviceIdType.MESH)
+    pl.semaphore_wait(barrier, 9)
+
+    def remote(src, dst, send, recv, device):
+        return pltpu.make_async_remote_copy(
+            src_ref=src, dst_ref=dst, send_sem=send, recv_sem=recv,
+            device_id=device, device_id_type=pl.DeviceIdType.MESH,
+        )
+
+    def first(o, b, h):
+        target = 2 * ((x + 1 + o) % 2) + b
+        src = tok.at[target, h]
+        dst = a.at[o, s, z, h]
+        zt = 2 * x + b
+        stays = (zt == z) & (x == h)
+        return (
+            stays,
+            remote(src, dst, s1s.at[o, b, h], s1r.at[o, z], (g, zt, h, s)),
+            pltpu.make_async_copy(src, dst, s1r.at[o, z]),
+        )
+
+    def start_first(o):
+        for b in range(2):
+            for h in range(2):
+                stays, away, local = first(o, b, h)
+                pl.when(jnp.logical_not(stays))(away.start)
+                pl.when(stays)(local.start)
+
+    def arrived(o, zs):
+        dst = a.at[o, s, zs, x]
+        local = (pair == x) & (z == zs)
+        pl.when(jnp.logical_not(local))(
+            remote(dst, dst, s1s.at[o, 0, 0], s1r.at[o, zs], x_mate).wait_recv
+        )
+        pl.when(local)(pltpu.make_async_copy(tok.at[0, 0], dst, s1r.at[o, zs]).wait)
+
+    def to_x(o, zs):
+        piece = a.at[o, s, zs, x]
+        return remote(piece, piece, s2s.at[o, zs], s2r.at[o, zs], x_mate)
+
+    def from_x(o, zs):
+        piece = a.at[o, s, zs, 1 - x]
+        return remote(piece, piece, s2s.at[o, zs], s2r.at[o, zs], x_mate)
+
+    def to_sub(o, zs):
+        piece = a.at[o, s, zs, x]
+        return remote(piece, piece, s3s.at[o, zs], s3r.at[o, zs], sibling)
+
+    def from_sub(o, zs):
+        piece = a.at[o, 1 - s, zs, x]
+        return remote(piece, piece, s3s.at[o, zs], s3r.at[o, zs], sibling)
+
+    def to_sub_late(o, zs):
+        piece = a.at[o, s, zs, 1 - x]
+        return remote(piece, piece, s4s.at[o, zs], s4r.at[o, zs], sibling)
+
+    def from_sub_late(o, zs):
+        piece = a.at[o, 1 - s, zs, 1 - x]
+        return remote(piece, piece, s4s.at[o, zs], s4r.at[o, zs], sibling)
+
+    def forward(o):
+        for zs in range(4):
+            arrived(o, zs)
+            to_x(o, zs).start()
+            to_sub(o, zs).start()
+        for zs in range(4):
+            from_x(o, zs).wait_recv()
+            to_sub_late(o, zs).start()
+        for zs in range(4):
+            from_sub(o, zs).wait_recv()
+            from_sub_late(o, zs).wait_recv()
+
+    def w_copy(c):
+        rows = pl.ds(pl.multiple_of(g * half, half), half)
+        return remote(w.at[c, rows], wm.at[c, rows], ws.at[c], wr.at[c], z_mate)
+
+    def w_forward(c):
+        rows = pl.ds(pl.multiple_of(g * half, half), half)
+        return remote(wm.at[c, rows], wm.at[c, rows], wfs.at[c], wfr.at[c], y_mate)
+
+    def w_forwarded(c):
+        rows = pl.ds(pl.multiple_of((1 - g) * half, half), half)
+        return remote(wm.at[c, rows], wm.at[c, rows], wfs.at[c], wfr.at[c], y_mate)
+
+    def p_copy(c):
+        return remote(psend.at[c], prec.at[c], ps.at[c], pr.at[c], far)
+
+    def s_copy():
+        return remote(ssend, srecv, ss.at[0], sr.at[0], far)
+
+    def kv_copy():
+        return remote(kvown, kvrecv, kvs.at[0], kvr.at[0], sibling)
+
+    def len_copy(step):
+        zt = (z + step) % 4
+        return remote(lens.at[zt], lrecv.at[z], ls.at[step], lr.at[step], (g, zt, x, s))
+
+    def product(o, c):
+        def tokens(block):
+            t = a[o, block]
+            return t.reshape(t.shape[0] * t.shape[1] * t.shape[2], t.shape[3])
+
+        return jnp.dot(
+            tokens(here), w[c], preferred_element_type=jnp.float32
+        ) + jnp.dot(tokens(1 - here), wm[c], preferred_element_type=jnp.float32)
+
+    def squares(o, zs, h):
+        total = None
+        for block in range(2):
+            t = a[o, block, zs, h].astype(jnp.float32)
+            part = jnp.sum(t * t, axis=1, keepdims=True)
+            total = part if total is None else total + part
+        return total
+
+    start_first(0)
+    for step in range(1, 4):
+        len_copy(step).start()
+    for c in range(n_chunks):
+        w_copy(c).start()
+    start_first(1)
+
+    forward(0)
+
+    piece_rows = a.shape[4]
+
+    @pl.loop(0, 8)
+    def _(i):
+        rows = pl.ds(pl.multiple_of(i * piece_rows, piece_rows), piece_rows)
+        ssend[rows, :] = jnp.broadcast_to(squares(0, i // 2, i % 2), (piece_rows, 128))
+
+    s_copy().start()
+
+    w_copy(0).wait_recv()
+    w_forward(0).start()
+
+    def send_partial(c):
+        w_forwarded(c).wait_recv()
+        psend[c] = product(0, c).astype(psend.dtype)
+        p_copy(c).start()
+
+    @pl.loop(1, n_chunks)
+    def _(c):
+        w_copy(c).wait_recv()
+        w_forward(c).start()
+        send_partial(c - 1)
+
+    send_partial(n_chunks - 1)
+
+    forward(1)
+
+    @pl.loop(0, n_chunks)
+    def _(c):
+        own[c] = product(1, c)
+
+    s_copy().wait_recv()
+
+    @pl.loop(0, 8)
+    def _(i):
+        rows = pl.ds(pl.multiple_of(i * piece_rows, piece_rows), piece_rows)
+        total = squares(1, i // 2, i % 2) + srecv[rows, :]
+        srecv[rows, :] = lax.rsqrt(total / (4 * a.shape[5]) + EPS)
+
+    scale = jnp.concatenate([srecv[...]] * (CHUNK // 128), axis=1)
+    p_copy(0).wait_recv()
+    kvown[...] = (own[0] + prec[0].astype(jnp.float32)) * scale
+    kv_copy().start()
+    kv_out[s] = kvown[...]
+
+    @pl.loop(1, n_chunks)
+    def _(c):
+        p_copy(c).wait_recv()
+        wide = jnp.concatenate([srecv[...]] * (CHUNK // 128), axis=1)
+        q_out[c - 1] = (own[c] + prec[c].astype(jnp.float32)) * wide
+
+    len_out[z] = lens[z]
+    for step in range(1, 4):
+        source = (z + 4 - step) % 4
+        remote(lrecv.at[source], lrecv.at[source], ls.at[step], lr.at[step], x_mate).wait_recv()
+        len_out[source] = lrecv[source]
+
+    kv_copy().wait_recv()
+    kv_out[1 - s] = kvrecv[...]
+
+    for o in range(2):
+        for b in range(2):
+            for h in range(2):
+                stays, away, _ = first(o, b, h)
+                pl.when(jnp.logical_not(stays))(away.wait_send)
+        for zs in range(4):
+            to_x(o, zs).wait_send()
+            to_sub(o, zs).wait_send()
+            to_sub_late(o, zs).wait_send()
+    for c in range(n_chunks):
+        w_copy(c).wait_send()
+        w_forward(c).wait_send()
+        p_copy(c).wait_send()
+    s_copy().wait_send()
+    kv_copy().wait_send()
+    for step in range(1, 4):
+        len_copy(step).wait_send()
+
+
+def exchange(tok, lens, w):
+    chunks, width, columns = w.shape
+    tokens = tok.shape[0] * tok.shape[1] * tok.shape[2]
+    dma = pltpu.SemaphoreType.DMA
+    vmem = pl.BlockSpec(memory_space=pltpu.VMEM)
+    f32 = jnp.float32
+    bf16 = jnp.bfloat16
+    return pl.pallas_call(
+        exchange_kernel,
+        out_shape=(
+            jax.ShapeDtypeStruct((chunks - 1, tokens, columns), f32),
+            jax.ShapeDtypeStruct((2, tokens, columns), f32),
+            jax.ShapeDtypeStruct(lens.shape, f32),
+        ),
+        in_specs=[pl.BlockSpec(memory_space=pl.ANY), vmem, vmem],
+        out_specs=(vmem, vmem, vmem),
+        scratch_shapes=[
+            pltpu.VMEM((2, 2, 4, 2, tok.shape[2], width), bf16),
+            pltpu.VMEM((chunks, width, columns), bf16),
+            pltpu.VMEM((chunks, tokens, columns), bf16),
+            pltpu.VMEM((chunks, tokens, columns), bf16),
+            pltpu.VMEM((chunks, tokens, columns), f32),
+            pltpu.VMEM((tokens, 128), f32),
+            pltpu.VMEM((tokens, 128), f32),
+            pltpu.VMEM((tokens, columns), f32),
+            pltpu.VMEM((tokens, columns), f32),
+            pltpu.VMEM(lens.shape, f32),
+            dma((2, 2, 2)), dma((2, 4)), dma((2, 4)), dma((2, 4)),
+            dma((2, 4)), dma((2, 4)), dma((2, 4)), dma((2, 4)),
+            dma((chunks,)), dma((chunks,)), dma((chunks,)), dma((chunks,)),
+            dma((chunks,)), dma((chunks,)), dma((1,)), dma((1,)),
+            dma((4,)), dma((4,)), dma((1,)), dma((1,)),
+        ],
+        compiler_params=pltpu.CompilerParams(
+            collective_id=0, has_side_effects=True, vmem_limit_bytes=48 << 20
+        ),
+        cost_estimate=pl.CostEstimate(
+            flops=8 * tokens * width * chunks * columns, bytes_accessed=1 << 24, transcendentals=0
+        ),
+        name="exchange",
+    )(tok, lens, w)
+
+
+def attend_kernel(q_ref, kv_ref, len_ref, cos_ref, sin_ref, qg_ref, kg_ref, k_out, v_out, ctx_out):
+    head = cos_ref.shape[1]
+    rows = cos_ref.shape[0]
+    seqs, share, _ = k_out.shape
+    length = rows // seqs
+    core = lax.axis_index("sub")
+    len_key = jnp.broadcast_to(len_ref[0, 0:1, :], (rows, rows))
+    len_query = len_key.T
+    row_ids = lax.broadcasted_iota(jnp.int32, (rows, rows), 0)
+    col_ids = lax.broadcasted_iota(jnp.int32, (rows, rows), 1)
+    key_pos = (col_ids % length).astype(jnp.float32)
+    query_pos = (row_ids % length).astype(jnp.float32)
+    allowed = (
+        (row_ids // length == col_ids // length) & (col_ids <= row_ids) & (key_pos < len_key)
+    )
+    live = query_pos < len_query
+    cos = cos_ref[...]
+    sin = sin_ref[...]
+
+    def norm_rope(t, gain):
+        mean = jnp.mean(t * t, axis=-1, keepdims=True)
+        t = t * lax.rsqrt(mean + EPS) * gain
+        return t * cos + pltpu.roll(t, head // 2, 1) * sin
+
+    def part(t):
+        t = t.reshape(seqs, length, head)
+        return jnp.where(core == 0, t[:, :share], t[:, share:])
+
+    kgain = kg_ref[...]
+    qgain = qg_ref[...]
+    n_groups = kv_ref.shape[2] // head
+    heads = q_ref.shape[0] * q_ref.shape[2] // head // n_groups
+    per_chunk = q_ref.shape[2] // head
+    for group in range(n_groups):
+        cols = slice(group * head, (group + 1) * head)
+        key = jnp.where(live, norm_rope(kv_ref[0, :, cols], kgain), 0.0)
+        value = jnp.where(live, kv_ref[1, :, cols], 0.0)
+        k_out[:, :, cols] = part(key).astype(k_out.dtype)
+        v_out[:, :, cols] = part(value).astype(v_out.dtype)
+        key = key.astype(jnp.bfloat16)
+        value = value.astype(jnp.bfloat16)
+        for h in range(heads):
+            n = group * heads + h
+            at = n % per_chunk * head
+            query = norm_rope(q_ref[n // per_chunk, :, at : at + head], qgain)
+            scores = lax.dot_general(
+                query.astype(jnp.bfloat16), key, (((1,), (1,)), ((), ())),
+                preferred_element_type=jnp.float32,
+            ) * head ** (-0.5)
+            weights = jnp.where(allowed, jnp.exp(scores), 0.0)
+            probs = weights / jnp.sum(weights, axis=-1, keepdims=True)
+            out = jnp.dot(probs.astype(jnp.bfloat16), value, preferred_element_type=jnp.float32)
+            ctx_out[:, n * head : (n + 1) * head] = jnp.where(live, out, 0.0).astype(ctx_out.dtype)
+
+
+def attend(q, kv, lens, query_gain, k_gain, length, share):
+    head = query_gain.shape[0]
+    chunks, tokens, columns = q.shape
+    blocks = lens.shape[0]
+    rows = tokens // blocks
+    seqs = rows // length
+    frequency = THETA ** (-(2.0 * jnp.arange(head // 2, dtype=jnp.float32)) / head)
+    positions = jnp.arange(rows, dtype=jnp.int32) % length
+    angle = positions.astype(jnp.float32)[:, None] * frequency[None, :]
+    cos = jnp.cos(angle)
+    sin = jnp.sin(angle)
+    whole = lambda *shape: pl.BlockSpec(shape, lambda i: (0,) * len(shape))
+    cache = jax.ShapeDtypeStruct((tokens // length, share, columns), jnp.bfloat16)
+    return pl.pallas_call(
+        attend_kernel,
+        grid=(blocks,),
+        out_shape=(cache, cache, jax.ShapeDtypeStruct((tokens, chunks * columns), jnp.bfloat16)),
+        in_specs=[
+            pl.BlockSpec((chunks, rows, columns), lambda i: (0, i, 0)),
+            pl.BlockSpec((2, rows, columns), lambda i: (0, i, 0)),
+            pl.BlockSpec((1,) + lens.shape[1:], lambda i: (i, 0, 0)),
+            whole(rows, head), whole(rows, head), whole(1, head), whole(1, head),
+        ],
+        out_specs=(
+            pl.BlockSpec((seqs, share, columns), lambda i: (i, 0, 0)),
+            pl.BlockSpec((seqs, share, columns), lambda i: (i, 0, 0)),
+            pl.BlockSpec((rows, chunks * columns), lambda i: (i, 0)),
+        ),
+        compiler_params=pltpu.CompilerParams(vmem_limit_bytes=32 << 20),
+        name="attend",
+    )(
+        q, kv, lens,
+        jnp.concatenate([cos, cos], axis=1), jnp.concatenate([-sin, sin], axis=1),
+        query_gain[None, :], k_gain[None, :],
+    )
+
+
+def paired_body(
+    hidden, seq_len, target_rank, in_gain, joined_projection_weight, query_gain, k_gain
+):
+    slots, length, width = hidden.shape
+    ranks = lax.axis_size("dp")
+    pair = slots // ranks
+    local = jnp.arange(slots, dtype=jnp.int32)
+    same_target = (target_rank[:, None] == target_rank[None, :]) & (local[None, :] < local[:, None])
+    position = target_rank * pair + jnp.sum(same_target.astype(jnp.int32), axis=1)
+    hits = local[:, None] == position[None, :]
+    source = jnp.sum(jnp.where(hits, local[None, :], 0), axis=1)
+    sent_length = jnp.sum(jnp.where(hits, seq_len[None, :], 0), axis=1)
+    tok = jnp.take(hidden, source, axis=0).reshape(ranks, 2, pair // 2 * length, width)
+    lens = jnp.broadcast_to(
+        sent_length.astype(jnp.float32).reshape(ranks, 1, pair, 1), (ranks, 8, pair, length)
+    ).reshape(ranks, 8, pair * length)
+
+    head = query_gain.shape[0]
+    rows, groups, span = joined_projection_weight.shape
+    group_query = span - 2 * head
+    query_cols = group_query // lax.axis_size("sub")
+    core = lax.axis_index("sub")
+    gain = lax.dynamic_slice_in_dim(in_gain, lax.axis_index("dp") * rows, rows, 0)
+    own_query = lax.dynamic_slice_in_dim(joined_projection_weight, core * query_cols, query_cols, 2)
+    own_kv = lax.dynamic_slice_in_dim(
+        joined_projection_weight, group_query + core * head, head, 2
+    )
+    columns = [own_kv[:, i] for i in range(groups)] + [own_query[:, i] for i in range(groups)]
+    flat = jnp.concatenate(columns, axis=1).astype(jnp.float32) * gain[:, None]
+    w = flat.astype(jnp.bfloat16).reshape(rows, -1, CHUNK).transpose(1, 0, 2)
+
+    q, kv, lengths = exchange(tok, lens, w)
+    share = length // lax.axis_size("sub")
+    key_share, value_share, context = attend(q, kv, lengths, query_gain, k_gain, length, share)
+    return (key_share, value_share, context.reshape(slots, length, groups, query_cols))
+
+
 def solution(mesh):
+    sizes = mesh.shape
+    paired = (
+        sizes["dp"] == 4 and sizes["tensor"] == 2 and sizes["sub"] == 2 and sizes["groups"] == 2
+    )
     placed = (
         P(("groups", "dp"), None, ("tensor", "sub")),
         P(("groups", "dp")),
@@ -134,7 +547,7 @@
         P(),
     )
     return jax.shard_map(
-        body,
+        paired_body if paired else body,
         mesh=mesh,
         in_specs=placed,
         out_specs=(

time: 344 us -> 190 us (0.55)
  waiting for transfers between devices: 223 us -> 0 us
  Pallas kernels: 0 us -> 146 us
  blocking collectives: 37.6 us -> 0 us
  matrix products: 15.5 us -> 0 us
  between operations: 14.3 us -> 0.78 us
  other arithmetic: 18.4 us -> 10.2 us
    all_gather x2 -> x0, waiting for transfers between devices: 218 us -> none  [the longest x1 213 us: body(): lax.all_gather(own_rows, ('dp', 'groups'), axis=0, tiled=True)]
    pallas_call x0 -> x2, Pallas kernels: none -> 146 us  [the longest x1 135 us: exchange(): pl.pallas_call(exchange_kernel, out_shape=(jax.ShapeDtypeStruct((chunks -...]
    all_to_all x1 -> x0, blocking collectives: 37.6 us -> none  [body(): lax.all_to_all(outgoing.reshape(ranks, pair, length, width), 'dp', split_...]
    convert_element_type x1 -> x3, local copies, waits for them, and re-layouts: 0.08 us -> 16.4 us  [the longest x2 16.3 us: paired_body(): flat = jnp.concatenate(columns, axis=1).astype(jnp.float32) * gain[:, None]]
    dot_general x3 -> x0, matrix products: 15.5 us -> none  [the longest x1 12.8 us: body(): jnp.dot(normed_query, lax.all_gather(own_rows, ('dp', 'groups'), axis=0,...]
    reshape x5 -> x1, local copies, waits for them, and re-layouts: 14.9 us -> 1.56 us  [paired_body(): context.reshape(slots, length, groups, query_cols)]
    slice x4 -> x2, local copies, waits for them, and re-layouts: 3.26 us -> 10.4 us  [the longest x1 7.68 us: paired_body(): own_query[:, i]]
    dynamic_slice x2 -> x1, local copies, waits for them, and re-layouts: 7.38 us -> 0.78 us  [paired_body(): lax.dynamic_slice_in_dim(in_gain, lax.axis_index('dp') * rows, rows, 0)]
  transfers between devices with their start and end apart: 3 -> 0, of which waited for: 3 -> 0; matrix products, arithmetic and copies ran while one was open for 9% -> 0% of each run, Pallas kernels for 0% -> 0%
where the time goes in v2:
time: 190 us
  Pallas kernels  146 us (77%)
  local copies, waits for them, and re-layouts  33.2 us (17%)
  other arithmetic  10.2 us (5%)
    pallas_call x1, Pallas kernels, exchange(): pl.pallas_call(exchange_kernel, out_shape=(jax.ShapeDtypeStruct((chunks -...  135 us
    convert_element_type x2, local copies, waits for them, and re-layouts, paired_body(): flat = jnp.concatenate(columns, axis=1).astype(jnp.float32) * gain[:, None]  16.3 us
    pallas_call x1, Pallas kernels, attend(): pl.pallas_call(attend_kernel, grid=(blocks,), out_shape=(cache, cache, ja...  10.2 us
    slice x1, local copies, waits for them, and re-layouts, paired_body(): own_query[:, i]  7.68 us
    transpose x1, other arithmetic, paired_body(): w = flat.astype(jnp.bfloat16).reshape(rows, -1, CHUNK).transpose(1, 0, 2)  4.99 us

profile of v2, /device:TPU:0, one launch (start us, length us, event | category | flops | bytes accessed | tf_op | source)
XLA Modules:
  0.0 189.8 jit_solution(9213409799379302781)
XLA Ops:
  0.6 0.0 copy-start
  0.6 7.7 %constant_dynamic-slice_fusion.3 = (bf16[1280,1,512]{2,1,0:T(2,128)(2,1)S(1)}, bf16[1280,1,512]{2,1,0:T(2,128)(2,1)S(1)}) fusion(bf16[1280,2,1280]{2,1,0:T(2,128)(2,1)} %param.11, s32[]{:T(128)S(6)} %select_n.61, s32[]{:T(128)S(6)} %add.53), kind=kLoop, calls=%fused_computation.28 | loop fusion | bytes 5242888 | tf_op jit(solution)/shard_map/slice | solution.py:525
  8.3 1.8 copy_bitcast_fusion
  10.2 0.0 copy-start.3
  10.2 2.7 %constant_dynamic-slice_fusion = (bf16[1280,1,128]{2,1,0:T(2,128)(2,1)S(1)}, bf16[1280,1,128]{2,1,0:T(2,128)(2,1)S(1)}) fusion(bf16[1280,2,1280]{2,1,0:T(2,128)(2,1)} %param.11, s32[]{:T(128)S(6)} %select_n.60, s32[]{:T(128)S(6)} %add.53), kind=kLoop, calls=%fused_computation.25 | loop fusion | bytes 1310728 | tf_op jit(solution)/shard_map/slice | solution.py:525
  12.9 0.1 copy_bitcast_fusion.2
  13.0 0.0 copy-done.3
  13.0 3.0 %maximum_convert_fusion = f32[1280,1280]{1,0:T(8,128)} fusion(bf16[1280,512]{1,0:T(8,128)(2,1)S(1)} %get-tuple-element.24, bf16[1280,512]{1,0:T(8,128)(2,1)S(1)} %copy-done.3, bf16[1280,128]{1,0:T(8,128)(2,1)S(1)} %get-tuple-element.26, bf16[1280,128]{1,0:T(8,128)(2,1)S(1)} %get-tuple-element.27), kind=kLoop, calls=%fused_computation.3 | loop fusion | flops 13107200 | bytes 9830400 | tf_op jit(solution)/shard_map/convert_element_type | solution.py:526
  15.9 8.2 %copy.22 = f32[1280,1280]{0,1:T(8,128)} copy(f32[1280,1280]{1,0:T(8,128)} %maximum_convert_fusion) | data formatting | bytes 13107200 | tf_op jit(solution)/shard_map/convert_element_type | solution.py:526
  24.1 8.2 %copy.23 = f32[1280,5,256]{2,0,1:T(8,128)} copy(f32[1280,5,256]{0,2,1:T(8,128)} %bitcast.22) | data formatting | bytes 13107200 | tf_op jit(solution)/shard_map/convert_element_type | solution.py:526
  32.3 0.8 dynamic_slice.11
  33.1 0.0 copy-start.5
  33.1 0.0 copy-start.4
  33.1 5.0 %fusion.w = bf16[5,1280,256]{2,1,0:T(8,128)(2,1)} fusion(f32[1280,5,256]{2,0,1:T(8,128)} %copy.23, f32[1280]{0:T(1024)S(1)} %dynamic_slice.11), kind=kLoop, calls=%fused_computation.2 | loop fusion | flops 3276800 | bytes 9835520 | tf_op jit(solution)/shard_map/transpose | solution.py:527
  38.1 0.0 copy-done.5
  38.1 0.2 convert_reduce_fusion
  38.3 0.0 copy-done.4
  38.3 0.1 select_reduce_fusion
  38.4 0.0 copy-done
  38.4 1.7 gather_fusion
  40.1 0.1 reduce_sum.33
  40.2 0.1 broadcast_in_dim.57
  40.3 0.1 broadcast_in_dim.58
  40.4 1.5 broadcast_select_fusion.tok
  41.9 0.1 convert_element_type.39
  42.0 0.1 broadcast_in_dim.62
  42.1 0.1 broadcast_in_dim.63
  42.2 0.0 copy-start.1
  42.2 0.0 copy-start.2
  42.2 135.4 %exchange.1 = (f32[4,512,256]{2,1,0:T(8,128)S(1)}, f32[2,512,256]{2,1,0:T(8,128)S(1)}, f32[4,8,128]{2,1,0:T(8,128)S(1)}) custom-call(bf16[4,2,64,1280]{3,2,1,0:T(8,128)(2,1)S(1)} %broadcast_select_fusion.tok, f32[4,8,128]{2,1,0:T(8,128)S(1)} %broadcast_in_dim.64.lens, bf16[5,1280,256]{2,1,0:T(8,128)(2,1)} %fusion.w), custom_call_target="tpu_custom_call" | custom-call | flops 6710886400 | bytes 16777216 | tf_op jit(solution)/shard_map/exchange/pallas_call | solution.py:370
  177.6 0.3 fusion.1
  177.9 0.1 pad_maximum_fusion
  178.0 0.0 copy-done.1
  178.0 0.0 copy-done.2
  178.0 10.2 %attend.1 = (bf16[16,16,256]{2,1,0:T(8,128)(2,1)}, bf16[16,16,256]{2,1,0:T(8,128)(2,1)}, bf16[512,1024]{1,0:T(8,128)(2,1)S(1)}) custom-call(f32[4,512,256]{2,1,0:T(8,128)S(1)} %get-tuple-element.9.q_ref, f32[2,512,256]{2,1,0:T(8,128)S(1)} %get-tuple-element.10.kv_ref, f32[4,8,128]{2,1,0:T(8,128)S(1)} %get-tuple-element.11.len_ref, ...), custom_call_target="tpu_custom_call" | custom-call | tf_op jit(solution)/shard_map/attend/pallas_call | solution.py:474
  188.3 1.6 reshape.73
  (10 shorter events, 0.1 us)
Async XLA Ops:
  0.6 37.8 %copy-start = (bf16[16,32,1280]{2,1,0:T(8,128)(2,1)S(1)}, bf16[16,32,1280]{2,1,0:T(8,128)(2,1)}, u32[]{:S(2)}) copy-start(bf16[16,32,1280]{2,1,0:T(8,128)(2,1)} %param.7) | copy-start | bytes 3932164
  10.2 2.8 %copy-start.3 = (bf16[1280,512]{1,0:T(8,128)(2,1)S(1)}, bf16[1280,512]{1,0:T(8,128)(2,1)}, u32[]{:S(2)}) copy-start(bf16[1280,512]{1,0:T(8,128)(2,1)} %get-tuple-element.25) | copy-start | bytes 3932164
  33.1 5.0 %copy-start.5 = (s32[16]{0:T(128)S(1)}, s32[16]{0:T(128)}, u32[]{:S(2)}) copy-start(s32[16]{0:T(128)} %param.9) | copy-start | bytes 196
  33.1 5.2 %copy-start.4 = (s32[16]{0:T(128)S(1)}, s32[16]{0:T(128)}, u32[]{:S(2)}) copy-start(s32[16]{0:T(128)} %param.8) | copy-start | bytes 196
  42.2 135.8 %copy-start.1 = (f32[128]{0:T(128)S(1)}, f32[128]{0:T(128)}, u32[]{:S(2)}) copy-start(f32[128]{0:T(128)} %param.12) | copy-start | bytes 1540
  42.2 135.8 %copy-start.2 = (f32[128]{0:T(128)S(1)}, f32[128]{0:T(128)}, u32[]{:S(2)}) copy-start(f32[128]{0:T(128)} %param.13) | copy-start | bytes 1540

commit v3 on v2

--- a/solution.py
+++ b/solution.py
@@ -132,7 +132,7 @@
 
 def exchange_kernel(
     tok, lens, w, q_out, kv_out, len_out,
-    a, wm, psend, prec, own, ssend, srecv, kvown, kvrecv, lrecv,
+    a, wm, psend, prec, own, ssend, srecv, scales, kvown, kvrecv, lrecv,
     s1s, s1r, s2s, s2r, s3s, s3r, s4s, s4r,
     ws, wr, wfs, wfr, ps, pr, ss, sr, ls, lr, kvs, kvr,
 ):
@@ -218,11 +218,12 @@
         piece = a.at[o, 1 - s, zs, 1 - x]
         return remote(piece, piece, s4s.at[o, zs], s4r.at[o, zs], sibling)
 
-    def forward(o):
+    def forward(o, after):
         for zs in range(4):
             arrived(o, zs)
             to_x(o, zs).start()
             to_sub(o, zs).start()
+        after()
         for zs in range(4):
             from_x(o, zs).wait_recv()
             to_sub_late(o, zs).start()
@@ -264,10 +265,10 @@
             tokens(here), w[c], preferred_element_type=jnp.float32
         ) + jnp.dot(tokens(1 - here), wm[c], preferred_element_type=jnp.float32)
 
-    def squares(o, zs, h):
+    def squares(o, zs):
         total = None
         for block in range(2):
-            t = a[o, block, zs, h].astype(jnp.float32)
+            t = a[o, block, zs].reshape(128, a.shape[5]).astype(jnp.float32)
             part = jnp.sum(t * t, axis=1, keepdims=True)
             total = part if total is None else total + part
         return total
@@ -275,20 +276,10 @@
     start_first(0)
     for step in range(1, 4):
         len_copy(step).start()
-    for c in range(n_chunks):
+    for c in range(2):
         w_copy(c).start()
-    start_first(1)
-
-    forward(0)
-
-    piece_rows = a.shape[4]
-
-    @pl.loop(0, 8)
-    def _(i):
-        rows = pl.ds(pl.multiple_of(i * piece_rows, piece_rows), piece_rows)
-        ssend[rows, :] = jnp.broadcast_to(squares(0, i // 2, i % 2), (piece_rows, 128))
-
-    s_copy().start()
+
+    forward(0, lambda: [w_copy(c).start() for c in range(2, n_chunks)])
 
     w_copy(0).wait_recv()
     w_forward(0).start()
@@ -302,11 +293,18 @@
     def _(c):
         w_copy(c).wait_recv()
         w_forward(c).start()
+        pl.when(c == n_chunks - 1)(lambda: start_first(1))
         send_partial(c - 1)
 
     send_partial(n_chunks - 1)
 
-    forward(1)
+    @pl.loop(0, 4)
+    def _(zs):
+        ssend[zs] = jnp.broadcast_to(squares(0, zs), (128, 128)).T[:8]
+
+    s_copy().start()
+
+    forward(1, lambda: None)
 
     @pl.loop(0, n_chunks)
     def _(c):
@@ -314,13 +312,13 @@
 
     s_copy().wait_recv()
 
-    @pl.loop(0, 8)
-    def _(i):
-        rows = pl.ds(pl.multiple_of(i * piece_rows, piece_rows), piece_rows)
-        total = squares(1, i // 2, i % 2) + srecv[rows, :]
-        srecv[rows, :] = lax.rsqrt(total / (4 * a.shape[5]) + EPS)
-
-    scale = jnp.concatenate([srecv[...]] * (CHUNK // 128), axis=1)
+    @pl.loop(0, 4)
+    def _(zs):
+        rows = pl.ds(pl.multiple_of(zs * 128, 128), 128)
+        total = squares(1, zs) + jnp.broadcast_to(srecv[zs, 0:1], (128, 128)).T
+        scales[rows, :] = lax.rsqrt(total / (4 * a.shape[5]) + EPS)
+
+    scale = jnp.concatenate([scales[...]] * (CHUNK // 128), axis=1)
     p_copy(0).wait_recv()
     kvown[...] = (own[0] + prec[0].astype(jnp.float32)) * scale
     kv_copy().start()
@@ -329,7 +327,7 @@
     @pl.loop(1, n_chunks)
     def _(c):
         p_copy(c).wait_recv()
-        wide = jnp.concatenate([srecv[...]] * (CHUNK // 128), axis=1)
+        wide = jnp.concatenate([scales[...]] * (CHUNK // 128), axis=1)
         q_out[c - 1] = (own[c] + prec[c].astype(jnp.float32)) * wide
 
     len_out[z] = lens[z]
@@ -382,7 +380,8 @@
             pltpu.VMEM((chunks, tokens, columns), bf16),
             pltpu.VMEM((chunks, tokens, columns), bf16),
             pltpu.VMEM((chunks, tokens, columns), f32),
-            pltpu.VMEM((tokens, 128), f32),
+            pltpu.VMEM(lens.shape, f32),
+            pltpu.VMEM(lens.shape, f32),
             pltpu.VMEM((tokens, 128), f32),
             pltpu.VMEM((tokens, columns), f32),
             pltpu.VMEM((tokens, columns), f32),
@@ -507,7 +506,7 @@
     hits = local[:, None] == position[None, :]
     source = jnp.sum(jnp.where(hits, local[None, :], 0), axis=1)
     sent_length = jnp.sum(jnp.where(hits, seq_len[None, :], 0), axis=1)
-    tok = jnp.take(hidden, source, axis=0).reshape(ranks, 2, pair // 2 * length, width)
+    tok = jnp.take(hidden, source, axis=0, mode="clip").reshape(ranks, 2, pair // 2 * length, width)
     lens = jnp.broadcast_to(
         sent_length.astype(jnp.float32).reshape(ranks, 1, pair, 1), (ranks, 8, pair, length)
     ).reshape(ranks, 8, pair * length)
@@ -522,9 +521,10 @@
     own_kv = lax.dynamic_slice_in_dim(
         joined_projection_weight, group_query + core * head, head, 2
     )
-    columns = [own_kv[:, i] for i in range(groups)] + [own_query[:, i] for i in range(groups)]
-    flat = jnp.concatenate(columns, axis=1).astype(jnp.float32) * gain[:, None]
-    w = flat.astype(jnp.bfloat16).reshape(rows, -1, CHUNK).transpose(1, 0, 2)
+    columns = [jnp.concatenate([own_kv[:, i] for i in range(groups)], axis=1)] + [
+        own_query[:, i, at : at + CHUNK] for i in range(groups) for at in range(0, query_cols, CHUNK)
+    ]
+    w = (jnp.stack(columns).astype(jnp.float32) * gain[None, :, None]).astype(jnp.bfloat16)
 
     q, kv, lengths = exchange(tok, lens, w)
     share = length // lax.axis_size("sub")

time: 190 us -> 184 us (0.968); the launches traced: 190 us -> 181 us
  local copies, waits for them, and re-layouts: 33.2 us -> 17.7 us
  Pallas kernels: 146 us -> 157 us
  other arithmetic: 10.2 us -> 5.94 us
    convert_element_type x2 -> x0, local copies, waits for them, and re-layouts: 16.3 us -> none  [paired_body(): flat = jnp.concatenate(columns, axis=1).astype(jnp.float32) * gain[:, None]]
    pallas_call x1, Pallas kernels: 135 us -> 147 us  [exchange(): pl.pallas_call(exchange_kernel, out_shape=(jax.ShapeDtypeStruct((chunks -...]
    transpose x1 -> x0, other arithmetic: 4.99 us -> none  [paired_body(): w = flat.astype(jnp.bfloat16).reshape(rows, -1, CHUNK).transpose(1, 0, 2)]
    unnamed x12 -> x13, local copies, waits for them, and re-layouts: 0.03 us -> 2.94 us
where the time goes in v3:
time: 184 us; the launch traced here: 181 us
  Pallas kernels  157 us (85%)
  local copies, waits for them, and re-layouts  17.7 us (10%)
  other arithmetic  5.94 us (3%)
    pallas_call x1, Pallas kernels, exchange(): pl.pallas_call(exchange_kernel, out_shape=(jax.ShapeDtypeStruct((chunks -...  147 us
    pallas_call x1, Pallas kernels, attend(): pl.pallas_call(attend_kernel, grid=(blocks,), out_shape=(cache, cache, ja...  10.2 us
    slice x1, local copies, waits for them, and re-layouts, paired_body(): own_query[:, i, at:at + CHUNK]  7.82 us
    convert_element_type x1, other arithmetic, paired_body(): (jnp.stack(columns).astype(jnp.float32) * gain[None, :, None]).astype(jnp...  4.28 us

profile of v3, /device:TPU:0, one launch (start us, length us, event | category | flops | bytes accessed | tf_op | source)
XLA Modules:
  0.0 181.3 jit_solution(15652066386359161790)
XLA Ops:
  0.6 0.0 copy-start
  0.7 2.7 %constant_dynamic-slice_fusion.2 = (bf16[1280,1,128]{2,1,0:T(2,128)(2,1)S(1)}, bf16[1280,1,128]{2,1,0:T(2,128)(2,1)S(1)}) fusion(bf16[1280,2,1280]{2,1,0:T(2,128)(2,1)} %param.11, s32[]{:T(128)S(6)} %select_n.35, s32[]{:T(128)S(6)} %add.35), kind=kLoop, calls=%fused_computation.29 | loop fusion | bytes 1310728 | tf_op jit(solution)/shard_map/slice | solution.py:524
  3.3 0.1 copy_bitcast_fusion.4
  3.4 0.9 fusion
  4.4 7.8 %constant_dynamic-slice_fusion.3 = (bf16[1280,1,256]{2,1,0:T(2,128)(2,1)S(1)}, bf16[1280,1,256]{2,1,0:T(2,128)(2,1)S(1)}, bf16[1280,1,256]{2,1,0:T(2,128)(2,1)S(1)}, bf16[1280,1,256]{2,1,0:T(2,128)(2,1)S(1)}) fusion(bf16[1280,2,1280]{2,1,0:T(2,128)(2,1)} %param.11, s32[]{:T(128)S(6)} %add.35, s32[]{:T(128)S(6)} %add.36, s32[]{:T(128)S(6)} %select_n.36), kind=kLoop, calls=%fused_computation.30 | loop fusion | bytes 5242892 | tf_op jit(solution)/shard_map/slice | solution.py:525
  12.2 1.0 fusion.4
  13.2 1.0 fusion.3
  14.1 1.0 fusion.2
  15.1 1.0 fusion.1
  16.1 0.8 dynamic_slice.11
  16.9 0.0 copy-start.4
  16.9 0.0 copy-start.3
  16.9 4.3 %multiply_convert_fusion.w = bf16[5,1280,256]{2,1,0:T(8,128)(2,1)} fusion(bf16[5,1280,256]{2,1,0:T(8,128)(2,1)} %fusion.1, f32[1280]{0:T(1024)S(1)} %dynamic_slice.11), kind=kLoop, calls=%fused_computation.1 | loop fusion | flops 4915200 | bytes 6558720 | tf_op jit(solution)/shard_map/convert_element_type | solution.py:527
  21.1 0.0 copy-done.4
  21.1 0.2 convert_reduce_fusion
  21.3 0.0 copy-done.3
  21.3 0.1 select_reduce_fusion
  21.5 0.0 copy-done
  21.5 0.6 gather_fusion
  22.1 0.1 convert_element_type.34
  22.2 0.1 broadcast_in_dim.49
  22.3 0.1 broadcast_in_dim.50
  22.4 0.0 copy-start.1
  22.4 0.0 copy-start.2
  22.4 146.6 %exchange.1 = (f32[4,512,256]{2,1,0:T(8,128)S(1)}, f32[2,512,256]{2,1,0:T(8,128)S(1)}, f32[4,8,128]{2,1,0:T(8,128)S(1)}) custom-call(bf16[4,2,64,1280]{3,2,1,0:T(8,128)(2,1)S(1)} %bitcast.27, f32[4,8,128]{2,1,0:T(8,128)S(1)} %broadcast_in_dim.51.lens, bf16[5,1280,256]{2,1,0:T(8,128)(2,1)} %multiply_convert_fusion.w), custom_call_target="tpu_custom_call" | custom-call | flops 6710886400 | bytes 16777216 | tf_op jit(solution)/shard_map/exchange/pallas_call | solution.py:368
  169.0 0.3 fusion.5
  169.3 0.1 pad_maximum_fusion
  169.4 0.0 copy-done.1
  169.5 0.0 copy-done.2
  169.5 10.2 %attend.1 = (bf16[16,16,256]{2,1,0:T(8,128)(2,1)}, bf16[16,16,256]{2,1,0:T(8,128)(2,1)}, bf16[512,1024]{1,0:T(8,128)(2,1)S(1)}) custom-call(f32[4,512,256]{2,1,0:T(8,128)S(1)} %get-tuple-element.9.q_ref, f32[2,512,256]{2,1,0:T(8,128)S(1)} %get-tuple-element.10.kv_ref, f32[4,8,128]{2,1,0:T(8,128)S(1)} %get-tuple-element.11.len_ref, ...), custom_call_target="tpu_custom_call" | custom-call | tf_op jit(solution)/shard_map/attend/pallas_call | solution.py:473
  179.7 1.6 reshape.44
  (6 shorter events, 0.0 us)
Async XLA Ops:
  0.6 20.8 %copy-start = (bf16[16,32,1280]{2,1,0:T(8,128)(2,1)S(1)}, bf16[16,32,1280]{2,1,0:T(8,128)(2,1)}, u32[]{:S(2)}) copy-start(bf16[16,32,1280]{2,1,0:T(8,128)(2,1)} %param.7) | copy-start | bytes 3932164
  16.9 4.3 %copy-start.4 = (s32[16]{0:T(128)S(1)}, s32[16]{0:T(128)}, u32[]{:S(2)}) copy-start(s32[16]{0:T(128)} %param.9) | copy-start | bytes 196
  16.9 4.5 %copy-start.3 = (s32[16]{0:T(128)S(1)}, s32[16]{0:T(128)}, u32[]{:S(2)}) copy-start(s32[16]{0:T(128)} %param.8) | copy-start | bytes 196
  22.4 147.1 %copy-start.1 = (f32[128]{0:T(128)S(1)}, f32[128]{0:T(128)}, u32[]{:S(2)}) copy-start(f32[128]{0:T(128)} %param.12) | copy-start | bytes 1540
  22.4 147.1 %copy-start.2 = (f32[128]{0:T(128)S(1)}, f32[128]{0:T(128)}, u32[]{:S(2)}) copy-start(f32[128]{0:T(128)} %param.13) | copy-start | bytes 1540

commit v4 on v3

--- a/solution.py
+++ b/solution.py
@@ -142,8 +142,8 @@
     s = lax.axis_index("sub")
     here = z % 2
     pair = z // 2
-    half = w.shape[1] // 2
-    n_chunks = w.shape[0]
+    half = w.shape[0] // 2
+    n_chunks = wm.shape[0]
     x_mate = (g, z, 1 - x, s)
     sibling = (g, z, x, 1 - s)
     z_mate = (g, pair * 2 + (1 - here), x, s)
@@ -218,22 +218,26 @@
         piece = a.at[o, 1 - s, zs, 1 - x]
         return remote(piece, piece, s4s.at[o, zs], s4r.at[o, zs], sibling)
 
-    def forward(o, after):
+    def forward_first(o):
         for zs in range(4):
             arrived(o, zs)
             to_x(o, zs).start()
             to_sub(o, zs).start()
-        after()
+
+    def forward_second(o):
         for zs in range(4):
             from_x(o, zs).wait_recv()
             to_sub_late(o, zs).start()
+
+    def forward_last(o):
         for zs in range(4):
             from_sub(o, zs).wait_recv()
             from_sub_late(o, zs).wait_recv()
 
     def w_copy(c):
         rows = pl.ds(pl.multiple_of(g * half, half), half)
-        return remote(w.at[c, rows], wm.at[c, rows], ws.at[c], wr.at[c], z_mate)
+        cols = pl.ds(pl.multiple_of(c * CHUNK, CHUNK), CHUNK)
+        return remote(w.at[rows, cols], wm.at[c, rows], ws.at[c], wr.at[c], z_mate)
 
     def w_forward(c):
         rows = pl.ds(pl.multiple_of(g * half, half), half)
@@ -261,8 +265,9 @@
             t = a[o, block]
             return t.reshape(t.shape[0] * t.shape[1] * t.shape[2], t.shape[3])
 
+        cols = pl.ds(pl.multiple_of(c * CHUNK, CHUNK), CHUNK)
         return jnp.dot(
-            tokens(here), w[c], preferred_element_type=jnp.float32
+            tokens(here), w[:, cols], preferred_element_type=jnp.float32
         ) + jnp.dot(tokens(1 - here), wm[c], preferred_element_type=jnp.float32)
 
     def squares(o, zs):
@@ -276,27 +281,24 @@
     start_first(0)
     for step in range(1, 4):
         len_copy(step).start()
-    for c in range(2):
+    for c in range(n_chunks):
         w_copy(c).start()
 
-    forward(0, lambda: [w_copy(c).start() for c in range(2, n_chunks)])
-
-    w_copy(0).wait_recv()
-    w_forward(0).start()
-
-    def send_partial(c):
+    forward_first(0)
+    start_first(1)
+    for c in range(n_chunks):
+        w_copy(c).wait_recv()
+        w_forward(c).start()
+    forward_second(0)
+    forward_last(0)
+
+    @pl.loop(0, n_chunks)
+    def _(c):
         w_forwarded(c).wait_recv()
         psend[c] = product(0, c).astype(psend.dtype)
         p_copy(c).start()
-
-    @pl.loop(1, n_chunks)
-    def _(c):
-        w_copy(c).wait_recv()
-        w_forward(c).start()
-        pl.when(c == n_chunks - 1)(lambda: start_first(1))
-        send_partial(c - 1)
-
-    send_partial(n_chunks - 1)
+        pl.when(c == 1)(lambda: forward_first(1))
+        pl.when(c == 2)(lambda: forward_second(1))
 
     @pl.loop(0, 4)
     def _(zs):
@@ -304,7 +306,7 @@
 
     s_copy().start()
 
-    forward(1, lambda: None)
+    forward_last(1)
 
     @pl.loop(0, n_chunks)
     def _(c):
@@ -359,7 +361,9 @@
 
 
 def exchange(tok, lens, w):
-    chunks, width, columns = w.shape
+    width = w.shape[0]
+    columns = CHUNK
+    chunks = w.shape[1] // columns
     tokens = tok.shape[0] * tok.shape[1] * tok.shape[2]
     dma = pltpu.SemaphoreType.DMA
     vmem = pl.BlockSpec(memory_space=pltpu.VMEM)
@@ -521,10 +525,9 @@
     own_kv = lax.dynamic_slice_in_dim(
         joined_projection_weight, group_query + core * head, head, 2
     )
-    columns = [jnp.concatenate([own_kv[:, i] for i in range(groups)], axis=1)] + [
-        own_query[:, i, at : at + CHUNK] for i in range(groups) for at in range(0, query_cols, CHUNK)
-    ]
-    w = (jnp.stack(columns).astype(jnp.float32) * gain[None, :, None]).astype(jnp.bfloat16)
+    columns = [own_kv[:, i] for i in range(groups)] + [own_query[:, i] for i in range(groups)]
+    flat = jnp.concatenate(columns, axis=1).astype(jnp.float32) * gain[:, None]
+    w = flat.astype(jnp.bfloat16)
 
     q, kv, lengths = exchange(tok, lens, w)
     share = length // lax.axis_size("sub")

time: 184 us -> 164 us (0.89); the launches traced: 181 us -> 163 us
  Pallas kernels: 157 us -> 143 us
  local copies, waits for them, and re-layouts: 17.7 us -> 15.4 us
  other arithmetic: 5.94 us -> 3.97 us
    pallas_call x1, Pallas kernels: 147 us -> 133 us  [exchange(): pl.pallas_call(exchange_kernel, out_shape=(jax.ShapeDtypeStruct((chunks -...]
    unnamed x13 -> x10, local copies, waits for them, and re-layouts: 2.94 us -> 0.02 us
where the time goes in v4:
time: 164 us; the launch traced here: 163 us
  Pallas kernels  143 us (87%)
  local copies, waits for them, and re-layouts  15.4 us (9%)
  other arithmetic  3.97 us (2%)
    pallas_call x1, Pallas kernels, exchange(): pl.pallas_call(exchange_kernel, out_shape=(jax.ShapeDtypeStruct((chunks -...  133 us
    pallas_call x1, Pallas kernels, attend(): pl.pallas_call(attend_kernel, grid=(blocks,), out_shape=(cache, cache, ja...  10.2 us
    slice x1, local copies, waits for them, and re-layouts, paired_body(): own_query[:, i]  7.58 us

profile of v4, /device:TPU:0, one launch (start us, length us, event | category | flops | bytes accessed | tf_op | source)
XLA Modules:
  0.0 163.4 jit_solution(14142525395030853002)
XLA Ops:
  0.6 0.0 copy-start
  0.6 7.6 %constant_dynamic-slice_fusion.3 = (bf16[1280,1,512]{2,1,0:T(2,128)(2,1)S(1)}, bf16[1280,1,512]{2,1,0:T(2,128)(2,1)S(1)}) fusion(bf16[1280,2,1280]{2,1,0:T(2,128)(2,1)} %param.11, s32[]{:T(128)S(6)} %select_n.36, s32[]{:T(128)S(6)} %add.35), kind=kLoop, calls=%fused_computation.22 | loop fusion | bytes 5242888 | tf_op jit(solution)/shard_map/slice | solution.py:528
  8.2 1.8 %copy_bitcast_fusion = (bf16[1280,512]{1,0:T(8,128)(2,1)S(1)}, bf16[1280,512]{1,0:T(8,128)(2,1)}) fusion(bf16[1280,1,512]{2,1,0:T(2,128)(2,1)S(1)} %get-tuple-element.20, bf16[1280,1,512]{2,1,0:T(2,128)(2,1)S(1)} %get-tuple-element.19), kind=kLoop, calls=%fused_computation.2 | loop fusion | bytes 5242880 | tf_op jit(solution)/shard_map/squeeze | solution.py:528
  10.1 2.7 %constant_dynamic-slice_fusion = (bf16[1280,1,128]{2,1,0:T(2,128)(2,1)S(1)}, bf16[1280,1,128]{2,1,0:T(2,128)(2,1)S(1)}) fusion(bf16[1280,2,1280]{2,1,0:T(2,128)(2,1)} %param.11, s32[]{:T(128)S(6)} %select_n.35, s32[]{:T(128)S(6)} %add.35), kind=kLoop, calls=%fused_computation.19 | loop fusion | bytes 1310728 | tf_op jit(solution)/shard_map/slice | solution.py:528
  12.7 0.1 copy_bitcast_fusion.2
  12.8 0.8 dynamic_slice.11
  13.6 0.0 copy-start.4
  13.6 0.0 copy-start.3
  13.6 3.2 %multiply_convert_fusion.w = bf16[1280,1280]{1,0:T(8,128)(2,1)} fusion(bf16[1280,512]{1,0:T(8,128)(2,1)S(1)} %get-tuple-element.24, bf16[1280,512]{1,0:T(8,128)(2,1)} %get-tuple-element.25, bf16[1280,128]{1,0:T(8,128)(2,1)S(1)} %get-tuple-element.26, bf16[1280,128]{1,0:T(8,128)(2,1)S(1)} %get-tuple-element.27, f32[1280]{0:T(1024)S(1)} %dynamic_slice.11), kind=kLoop, calls=%fused_computation.1 | loop fusion | flops 16384000 | bytes 6558720 | tf_op jit(solution)/shard_map/convert_element_type | solution.py:530
  16.9 0.0 copy-done.4
  16.9 0.2 convert_reduce_fusion
  17.1 0.0 copy-done.3
  17.1 0.1 select_reduce_fusion
  17.2 0.0 copy-done
  17.2 0.6 gather_fusion
  17.9 0.1 convert_element_type.34
  17.9 0.1 broadcast_in_dim.49
  18.0 0.1 broadcast_in_dim.50
  18.1 0.0 copy-start.1
  18.1 0.0 copy-start.2
  18.1 133.0 %exchange.1 = (f32[4,512,256]{2,1,0:T(8,128)S(1)}, f32[2,512,256]{2,1,0:T(8,128)S(1)}, f32[4,8,128]{2,1,0:T(8,128)S(1)}) custom-call(bf16[4,2,64,1280]{3,2,1,0:T(8,128)(2,1)S(1)} %bitcast.11, f32[4,8,128]{2,1,0:T(8,128)S(1)} %broadcast_in_dim.51.lens, bf16[1280,1280]{1,0:T(8,128)(2,1)} %multiply_convert_fusion.w), custom_call_target="tpu_custom_call" | custom-call | flops 6710886400 | bytes 16777216 | tf_op jit(solution)/shard_map/exchange/pallas_call | solution.py:372
  151.2 0.3 fusion
  151.5 0.1 pad_maximum_fusion
  151.6 0.0 copy-done.1
  151.6 0.0 copy-done.2
  151.6 10.2 %attend.1 = (bf16[16,16,256]{2,1,0:T(8,128)(2,1)}, bf16[16,16,256]{2,1,0:T(8,128)(2,1)}, bf16[512,1024]{1,0:T(8,128)(2,1)S(1)}) custom-call(f32[4,512,256]{2,1,0:T(8,128)S(1)} %get-tuple-element.9.q_ref, f32[2,512,256]{2,1,0:T(8,128)S(1)} %get-tuple-element.10.kv_ref, f32[4,8,128]{2,1,0:T(8,128)S(1)} %get-tuple-element.11.len_ref, ...), custom_call_target="tpu_custom_call" | custom-call | tf_op jit(solution)/shard_map/attend/pallas_call | solution.py:477
  161.9 1.6 reshape.44
  (6 shorter events, 0.0 us)
Async XLA Ops:
  0.6 16.6 %copy-start = (bf16[16,32,1280]{2,1,0:T(8,128)(2,1)S(1)}, bf16[16,32,1280]{2,1,0:T(8,128)(2,1)}, u32[]{:S(2)}) copy-start(bf16[16,32,1280]{2,1,0:T(8,128)(2,1)} %param.7) | copy-start | bytes 3932164
  13.6 3.2 %copy-start.4 = (s32[16]{0:T(128)S(1)}, s32[16]{0:T(128)}, u32[]{:S(2)}) copy-start(s32[16]{0:T(128)} %param.9) | copy-start | bytes 196
  13.6 3.4 %copy-start.3 = (s32[16]{0:T(128)S(1)}, s32[16]{0:T(128)}, u32[]{:S(2)}) copy-start(s32[16]{0:T(128)} %param.8) | copy-start | bytes 196
  18.1 133.5 %copy-start.1 = (f32[128]{0:T(128)S(1)}, f32[128]{0:T(128)}, u32[]{:S(2)}) copy-start(f32[128]{0:T(128)} %param.12) | copy-start | bytes 1540
  18.1 133.5 %copy-start.2 = (f32[128]{0:T(128)S(1)}, f32[128]{0:T(128)}, u32[]{:S(2)}) copy-start(f32[128]{0:T(128)} %param.13) | copy-start | bytes 1540

commit v5 on v4

--- a/solution.py
+++ b/solution.py
@@ -281,24 +281,32 @@
     start_first(0)
     for step in range(1, 4):
         len_copy(step).start()
-    for c in range(n_chunks):
+    for c in range(2):
         w_copy(c).start()
 
     forward_first(0)
+    for c in range(2, n_chunks):
+        w_copy(c).start()
     start_first(1)
-    for c in range(n_chunks):
-        w_copy(c).wait_recv()
-        w_forward(c).start()
+    w_copy(0).wait_recv()
+    w_forward(0).start()
     forward_second(0)
     forward_last(0)
 
-    @pl.loop(0, n_chunks)
-    def _(c):
+    def send_partial(c):
         w_forwarded(c).wait_recv()
         psend[c] = product(0, c).astype(psend.dtype)
         p_copy(c).start()
-        pl.when(c == 1)(lambda: forward_first(1))
-        pl.when(c == 2)(lambda: forward_second(1))
+
+    @pl.loop(1, n_chunks)
+    def _(c):
+        w_copy(c).wait_recv()
+        w_forward(c).start()
+        send_partial(c - 1)
+        pl.when(c == n_chunks - 2)(lambda: forward_first(1))
+        pl.when(c == n_chunks - 1)(lambda: forward_second(1))
+
+    send_partial(n_chunks - 1)
 
     @pl.loop(0, 4)
     def _(zs):

time: 164 us -> 159 us (0.970)
  Pallas kernels: 143 us -> 139 us
    pallas_call x1, Pallas kernels: 133 us -> 128 us  [exchange(): pl.pallas_call(exchange_kernel, out_shape=(jax.ShapeDtypeStruct((chunks -...]
where the time goes in v5:
time: 159 us
  Pallas kernels  139 us (87%)
  local copies, waits for them, and re-layouts  15.4 us (10%)
  other arithmetic  3.97 us (2%)
    pallas_call x1, Pallas kernels, exchange(): pl.pallas_call(exchange_kernel, out_shape=(jax.ShapeDtypeStruct((chunks -...  128 us
    pallas_call x1, Pallas kernels, attend(): pl.pallas_call(attend_kernel, grid=(blocks,), out_shape=(cache, cache, ja...  10.2 us
    slice x1, local copies, waits for them, and re-layouts, paired_body(): own_query[:, i]  7.58 us
    convert_element_type x1, other arithmetic, paired_body(): w = flat.astype(jnp.bfloat16)  3.23 us

profile of v5, /device:TPU:0, one launch (start us, length us, event | category | flops | bytes accessed | tf_op | source)
XLA Modules:
  0.0 158.7 jit_solution(10573574526749558098)
XLA Ops:
  0.6 0.0 copy-start
  0.6 7.6 %constant_dynamic-slice_fusion.3 = (bf16[1280,1,512]{2,1,0:T(2,128)(2,1)S(1)}, bf16[1280,1,512]{2,1,0:T(2,128)(2,1)S(1)}) fusion(bf16[1280,2,1280]{2,1,0:T(2,128)(2,1)} %param.11, s32[]{:T(128)S(6)} %select_n.36, s32[]{:T(128)S(6)} %add.35), kind=kLoop, calls=%fused_computation.22 | loop fusion | bytes 5242888 | tf_op jit(solution)/shard_map/slice | solution.py:536
  8.2 1.8 %copy_bitcast_fusion = (bf16[1280,512]{1,0:T(8,128)(2,1)S(1)}, bf16[1280,512]{1,0:T(8,128)(2,1)}) fusion(bf16[1280,1,512]{2,1,0:T(2,128)(2,1)S(1)} %get-tuple-element.20, bf16[1280,1,512]{2,1,0:T(2,128)(2,1)S(1)} %get-tuple-element.19), kind=kLoop, calls=%fused_computation.2 | loop fusion | bytes 5242880 | tf_op jit(solution)/shard_map/squeeze | solution.py:536
  10.1 2.7 %constant_dynamic-slice_fusion = (bf16[1280,1,128]{2,1,0:T(2,128)(2,1)S(1)}, bf16[1280,1,128]{2,1,0:T(2,128)(2,1)S(1)}) fusion(bf16[1280,2,1280]{2,1,0:T(2,128)(2,1)} %param.11, s32[]{:T(128)S(6)} %select_n.35, s32[]{:T(128)S(6)} %add.35), kind=kLoop, calls=%fused_computation.19 | loop fusion | bytes 1310728 | tf_op jit(solution)/shard_map/slice | solution.py:536
  12.7 0.1 copy_bitcast_fusion.2
  12.8 0.8 dynamic_slice.11
  13.6 0.0 copy-start.4
  13.6 0.0 copy-start.3
  13.6 3.2 %multiply_convert_fusion.w = bf16[1280,1280]{1,0:T(8,128)(2,1)} fusion(bf16[1280,512]{1,0:T(8,128)(2,1)S(1)} %get-tuple-element.24, bf16[1280,512]{1,0:T(8,128)(2,1)} %get-tuple-element.25, bf16[1280,128]{1,0:T(8,128)(2,1)S(1)} %get-tuple-element.26, bf16[1280,128]{1,0:T(8,128)(2,1)S(1)} %get-tuple-element.27, f32[1280]{0:T(1024)S(1)} %dynamic_slice.11), kind=kLoop, calls=%fused_computation.1 | loop fusion | flops 16384000 | bytes 6558720 | tf_op jit(solution)/shard_map/convert_element_type | solution.py:538
  16.9 0.0 copy-done.4
  16.9 0.2 convert_reduce_fusion
  17.1 0.0 copy-done.3
  17.1 0.1 select_reduce_fusion
  17.2 0.0 copy-done
  17.2 0.6 gather_fusion
  17.9 0.1 convert_element_type.34
  17.9 0.1 broadcast_in_dim.49
  18.0 0.1 broadcast_in_dim.50
  18.1 0.0 copy-start.1
  18.1 0.0 copy-start.2
  18.1 128.3 %exchange.1 = (f32[4,512,256]{2,1,0:T(8,128)S(1)}, f32[2,512,256]{2,1,0:T(8,128)S(1)}, f32[4,8,128]{2,1,0:T(8,128)S(1)}) custom-call(bf16[4,2,64,1280]{3,2,1,0:T(8,128)(2,1)S(1)} %bitcast.11, f32[4,8,128]{2,1,0:T(8,128)S(1)} %broadcast_in_dim.51.lens, bf16[1280,1280]{1,0:T(8,128)(2,1)} %multiply_convert_fusion.w), custom_call_target="tpu_custom_call" | custom-call | flops 6710886400 | bytes 16777216 | tf_op jit(solution)/shard_map/exchange/pallas_call | solution.py:380
  146.4 0.3 fusion
  146.7 0.1 pad_maximum_fusion
  146.8 0.0 copy-done.1
  146.9 0.0 copy-done.2
  146.9 10.2 %attend.1 = (bf16[16,16,256]{2,1,0:T(8,128)(2,1)}, bf16[16,16,256]{2,1,0:T(8,128)(2,1)}, bf16[512,1024]{1,0:T(8,128)(2,1)S(1)}) custom-call(f32[4,512,256]{2,1,0:T(8,128)S(1)} %get-tuple-element.9.q_ref, f32[2,512,256]{2,1,0:T(8,128)S(1)} %get-tuple-element.10.kv_ref, f32[4,8,128]{2,1,0:T(8,128)S(1)} %get-tuple-element.11.len_ref, ...), custom_call_target="tpu_custom_call" | custom-call | tf_op jit(solution)/shard_map/attend/pallas_call | solution.py:485
  157.1 1.6 reshape.44
  (6 shorter events, 0.0 us)
Async XLA Ops:
  0.6 16.6 %copy-start = (bf16[16,32,1280]{2,1,0:T(8,128)(2,1)S(1)}, bf16[16,32,1280]{2,1,0:T(8,128)(2,1)}, u32[]{:S(2)}) copy-start(bf16[16,32,1280]{2,1,0:T(8,128)(2,1)} %param.7) | copy-start | bytes 3932164
  13.6 3.2 %copy-start.4 = (s32[16]{0:T(128)S(1)}, s32[16]{0:T(128)}, u32[]{:S(2)}) copy-start(s32[16]{0:T(128)} %param.9) | copy-start | bytes 196
  13.6 3.4 %copy-start.3 = (s32[16]{0:T(128)S(1)}, s32[16]{0:T(128)}, u32[]{:S(2)}) copy-start(s32[16]{0:T(128)} %param.8) | copy-start | bytes 196
  18.1 128.7 %copy-start.1 = (f32[128]{0:T(128)S(1)}, f32[128]{0:T(128)}, u32[]{:S(2)}) copy-start(f32[128]{0:T(128)} %param.12) | copy-start | bytes 1540
  18.1 128.8 %copy-start.2 = (f32[128]{0:T(128)S(1)}, f32[128]{0:T(128)}, u32[]{:S(2)}) copy-start(f32[128]{0:T(128)} %param.13) | copy-start | bytes 1540

commit v6 on v5

--- a/solution.py
+++ b/solution.py
@@ -132,7 +132,8 @@
 
 def exchange_kernel(
     tok, lens, w, q_out, kv_out, len_out,
-    a, wm, psend, prec, own, ssend, srecv, scales, kvown, kvrecv, lrecv,
+    a, wm, psend, prec, own, ssend, srecv, scales, kvown, kvrecv, lrecv, relay,
+    rs, rr, fs,
     s1s, s1r, s2s, s2r, s3s, s3r, s4s, s4r,
     ws, wr, wfs, wfr, ps, pr, ss, sr, ls, lr, kvs, kvr,
 ):
@@ -167,24 +168,40 @@
             device_id=device, device_id_type=pl.DeviceIdType.MESH,
         )
 
-    def first(o, b, h):
+    def first(o, b):
         target = 2 * ((x + 1 + o) % 2) + b
-        src = tok.at[target, h]
-        dst = a.at[o, s, z, h]
         zt = 2 * x + b
-        stays = (zt == z) & (x == h)
+        near, across = tok.at[target, x], tok.at[target, 1 - x]
         return (
-            stays,
-            remote(src, dst, s1s.at[o, b, h], s1r.at[o, z], (g, zt, h, s)),
-            pltpu.make_async_copy(src, dst, s1r.at[o, z]),
+            zt == z,
+            remote(near, a.at[o, s, z, x], s1s.at[o, b, 0], s1r.at[o, z], (g, zt, x, s)),
+            pltpu.make_async_copy(near, a.at[o, s, z, x], s1r.at[o, z]),
+            remote(across, a.at[o, s, z, 1 - x], s1s.at[o, b, 1], s1r.at[o, z], x_mate),
+            remote(across, relay.at[o, b], rs.at[o, b], rr.at[o, b], x_mate),
         )
 
     def start_first(o):
         for b in range(2):
-            for h in range(2):
-                stays, away, local = first(o, b, h)
-                pl.when(jnp.logical_not(stays))(away.start)
-                pl.when(stays)(local.start)
+            stays, away, local, beside, over = first(o, b)
+            pl.when(jnp.logical_not(stays))(over.start)
+            pl.when(stays)(beside.start)
+            pl.when(jnp.logical_not(stays))(away.start)
+            pl.when(stays)(local.start)
+
+    def onward(o, b):
+        zt = 2 * (1 - x) + b
+        return zt != z, remote(
+            relay.at[o, b], a.at[o, s, z, x], fs.at[o, b], s1r.at[o, z], (g, zt, x, s)
+        )
+
+    def pass_on(o):
+        for b in range(2):
+            leaves, copy = onward(o, b)
+
+            @pl.when(leaves)
+            def _():
+                remote(relay.at[o, b], relay.at[o, b], rs.at[o, b], rr.at[o, b], x_mate).wait_recv()
+                copy.start()
 
     def arrived(o, zs):
         dst = a.at[o, s, zs, x]
@@ -284,12 +301,14 @@
     for c in range(2):
         w_copy(c).start()
 
+    pass_on(0)
     forward_first(0)
     for c in range(2, n_chunks):
         w_copy(c).start()
     start_first(1)
     w_copy(0).wait_recv()
     w_forward(0).start()
+    pass_on(1)
     forward_second(0)
     forward_last(0)
 
@@ -351,9 +370,12 @@
 
     for o in range(2):
         for b in range(2):
-            for h in range(2):
-                stays, away, _ = first(o, b, h)
-                pl.when(jnp.logical_not(stays))(away.wait_send)
+            stays, away, _, beside, over = first(o, b)
+            pl.when(jnp.logical_not(stays))(over.wait_send)
+            pl.when(stays)(beside.wait_send)
+            pl.when(jnp.logical_not(stays))(away.wait_send)
+            leaves, copy = onward(o, b)
+            pl.when(leaves)(copy.wait_send)
         for zs in range(4):
             to_x(o, zs).wait_send()
             to_sub(o, zs).wait_send()
@@ -398,6 +420,8 @@
             pltpu.VMEM((tokens, columns), f32),
             pltpu.VMEM((tokens, columns), f32),
             pltpu.VMEM(lens.shape, f32),
+            pltpu.VMEM((2, 2, tok.shape[2], width), bf16),
+            dma((2, 2)), dma((2, 2)), dma((2, 2)),
             dma((2, 2, 2)), dma((2, 4)), dma((2, 4)), dma((2, 4)),
             dma((2, 4)), dma((2, 4)), dma((2, 4)), dma((2, 4)),
             dma((chunks,)), dma((chunks,)), dma((chunks,)), dma((chunks,)),

time: 159 us -> 158 us (level)
  the two profiles are of different devices: /device:TPU:0 before, /device:TPU:25 now
where the time goes in v6:
time: 158 us; the launch traced here: 157 us
  Pallas kernels  137 us (87%)
  local copies, waits for them, and re-layouts  15.5 us (10%)
  other arithmetic  3.97 us (3%)
    pallas_call x1, Pallas kernels, exchange(): pl.pallas_call(exchange_kernel, out_shape=(jax.ShapeDtypeStruct((chunks -...  127 us
    pallas_call x1, Pallas kernels, attend(): pl.pallas_call(attend_kernel, grid=(blocks,), out_shape=(cache, cache, ja...  10.2 us
    slice x1, local copies, waits for them, and re-layouts, paired_body(): own_query[:, i]  7.69 us
    convert_element_type x1, other arithmetic, paired_body(): w = flat.astype(jnp.bfloat16)  3.23 us

profile of v6, /device:TPU:25, one launch (start us, length us, event | category | flops | bytes accessed | tf_op | source)
XLA Modules:
  0.0 157.4 jit_solution(17155583793905194020)
XLA Ops:
  0.6 0.0 copy-start
  0.6 7.7 %constant_dynamic-slice_fusion.3 = (bf16[1280,1,512]{2,1,0:T(2,128)(2,1)S(1)}, bf16[1280,1,512]{2,1,0:T(2,128)(2,1)S(1)}) fusion(bf16[1280,2,1280]{2,1,0:T(2,128)(2,1)} %param.11, s32[]{:T(128)S(6)} %select_n.36, s32[]{:T(128)S(6)} %add.35), kind=kLoop, calls=%fused_computation.22 | loop fusion | bytes 5242888 | tf_op jit(solution)/shard_map/slice | solution.py:560
  8.4 1.8 %copy_bitcast_fusion = (bf16[1280,512]{1,0:T(8,128)(2,1)S(1)}, bf16[1280,512]{1,0:T(8,128)(2,1)}) fusion(bf16[1280,1,512]{2,1,0:T(2,128)(2,1)S(1)} %get-tuple-element.20, bf16[1280,1,512]{2,1,0:T(2,128)(2,1)S(1)} %get-tuple-element.19), kind=kLoop, calls=%fused_computation.2 | loop fusion | bytes 5242880 | tf_op jit(solution)/shard_map/squeeze | solution.py:560
  10.2 2.7 %constant_dynamic-slice_fusion = (bf16[1280,1,128]{2,1,0:T(2,128)(2,1)S(1)}, bf16[1280,1,128]{2,1,0:T(2,128)(2,1)S(1)}) fusion(bf16[1280,2,1280]{2,1,0:T(2,128)(2,1)} %param.11, s32[]{:T(128)S(6)} %select_n.35, s32[]{:T(128)S(6)} %add.35), kind=kLoop, calls=%fused_computation.19 | loop fusion | bytes 1310728 | tf_op jit(solution)/shard_map/slice | solution.py:560
  12.8 0.1 copy_bitcast_fusion.2
  12.9 0.8 dynamic_slice.11
  13.7 0.0 copy-start.4
  13.7 0.0 copy-start.3
  13.7 3.2 %multiply_convert_fusion.w = bf16[1280,1280]{1,0:T(8,128)(2,1)} fusion(bf16[1280,512]{1,0:T(8,128)(2,1)S(1)} %get-tuple-element.24, bf16[1280,512]{1,0:T(8,128)(2,1)} %get-tuple-element.25, bf16[1280,128]{1,0:T(8,128)(2,1)S(1)} %get-tuple-element.26, bf16[1280,128]{1,0:T(8,128)(2,1)S(1)} %get-tuple-element.27, f32[1280]{0:T(1024)S(1)} %dynamic_slice.11), kind=kLoop, calls=%fused_computation.1 | loop fusion | flops 16384000 | bytes 6558720 | tf_op jit(solution)/shard_map/convert_element_type | solution.py:562
  17.0 0.0 copy-done.4
  17.0 0.2 convert_reduce_fusion
  17.2 0.0 copy-done.3
  17.2 0.1 select_reduce_fusion
  17.3 0.0 copy-done
  17.3 0.6 gather_fusion
  17.9 0.1 convert_element_type.34
  18.0 0.1 broadcast_in_dim.49
  18.1 0.1 broadcast_in_dim.50
  18.2 0.0 copy-start.1
  18.2 0.0 copy-start.2
  18.2 126.9 %exchange.1 = (f32[4,512,256]{2,1,0:T(8,128)S(1)}, f32[2,512,256]{2,1,0:T(8,128)S(1)}, f32[4,8,128]{2,1,0:T(8,128)S(1)}) custom-call(bf16[4,2,64,1280]{3,2,1,0:T(8,128)(2,1)S(1)} %bitcast.11, f32[4,8,128]{2,1,0:T(8,128)S(1)} %broadcast_in_dim.51.lens, bf16[1280,1280]{1,0:T(8,128)(2,1)} %multiply_convert_fusion.w), custom_call_target="tpu_custom_call" | custom-call | flops 6710886400 | bytes 16777216 | tf_op jit(solution)/shard_map/exchange/pallas_call | solution.py:402
  145.1 0.3 fusion
  145.5 0.1 pad_maximum_fusion
  145.6 0.0 copy-done.1
  145.6 0.0 copy-done.2
  145.6 10.2 %attend.1 = (bf16[16,16,256]{2,1,0:T(8,128)(2,1)}, bf16[16,16,256]{2,1,0:T(8,128)(2,1)}, bf16[512,1024]{1,0:T(8,128)(2,1)S(1)}) custom-call(f32[4,512,256]{2,1,0:T(8,128)S(1)} %get-tuple-element.9.q_ref, f32[2,512,256]{2,1,0:T(8,128)S(1)} %get-tuple-element.10.kv_ref, f32[4,8,128]{2,1,0:T(8,128)S(1)} %get-tuple-element.11.len_ref, ...), custom_call_target="tpu_custom_call" | custom-call | tf_op jit(solution)/shard_map/attend/pallas_call | solution.py:509
  155.8 1.6 reshape.44
  (6 shorter events, 0.0 us)
Async XLA Ops:
  0.6 16.7 %copy-start = (bf16[16,32,1280]{2,1,0:T(8,128)(2,1)S(1)}, bf16[16,32,1280]{2,1,0:T(8,128)(2,1)}, u32[]{:S(2)}) copy-start(bf16[16,32,1280]{2,1,0:T(8,128)(2,1)} %param.7) | copy-start | bytes 3932164
  13.7 3.2 %copy-start.4 = (s32[16]{0:T(128)S(1)}, s32[16]{0:T(128)}, u32[]{:S(2)}) copy-start(s32[16]{0:T(128)} %param.9) | copy-start | bytes 196
  13.7 3.4 %copy-start.3 = (s32[16]{0:T(128)S(1)}, s32[16]{0:T(128)}, u32[]{:S(2)}) copy-start(s32[16]{0:T(128)} %param.8) | copy-start | bytes 196
  18.2 127.4 %copy-start.1 = (f32[128]{0:T(128)S(1)}, f32[128]{0:T(128)}, u32[]{:S(2)}) copy-start(f32[128]{0:T(128)} %param.12) | copy-start | bytes 1540
  18.2 127.4 %copy-start.2 = (f32[128]{0:T(128)S(1)}, f32[128]{0:T(128)}, u32[]{:S(2)}) copy-start(f32[128]{0:T(128)} %param.13) | copy-start | bytes 1540

commit v7 on v6

--- a/solution.py
+++ b/solution.py
@@ -298,10 +298,10 @@
     start_first(0)
     for step in range(1, 4):
         len_copy(step).start()
+    pass_on(0)
     for c in range(2):
         w_copy(c).start()
 
-    pass_on(0)
     forward_first(0)
     for c in range(2, n_chunks):
         w_copy(c).start()

time: 158 us -> 146 us (0.924)
  Pallas kernels: 137 us -> 126 us
    pallas_call x1, Pallas kernels: 127 us -> 115 us  [exchange(): pl.pallas_call(exchange_kernel, out_shape=(jax.ShapeDtypeStruct((chunks -...]
where the time goes in v7:
time: 146 us
  Pallas kernels  126 us (86%)
  local copies, waits for them, and re-layouts  15.5 us (11%)
  other arithmetic  3.97 us (3%)
    pallas_call x1, Pallas kernels, exchange(): pl.pallas_call(exchange_kernel, out_shape=(jax.ShapeDtypeStruct((chunks -...  115 us
    pallas_call x1, Pallas kernels, attend(): pl.pallas_call(attend_kernel, grid=(blocks,), out_shape=(cache, cache, ja...  10.2 us
    slice x1, local copies, waits for them, and re-layouts, paired_body(): own_query[:, i]  7.69 us
    convert_element_type x1, other arithmetic, paired_body(): w = flat.astype(jnp.bfloat16)  3.23 us

profile of v7, /device:TPU:25, one launch (start us, length us, event | category | flops | bytes accessed | tf_op | source)
XLA Modules:
  0.0 145.8 jit_solution(11929528328266744666)
XLA Ops:
  0.6 0.0 copy-start
  0.6 7.7 %constant_dynamic-slice_fusion.3 = (bf16[1280,1,512]{2,1,0:T(2,128)(2,1)S(1)}, bf16[1280,1,512]{2,1,0:T(2,128)(2,1)S(1)}) fusion(bf16[1280,2,1280]{2,1,0:T(2,128)(2,1)} %param.11, s32[]{:T(128)S(6)} %select_n.36, s32[]{:T(128)S(6)} %add.35), kind=kLoop, calls=%fused_computation.22 | loop fusion | bytes 5242888 | tf_op jit(solution)/shard_map/slice | solution.py:560
  8.4 1.8 %copy_bitcast_fusion = (bf16[1280,512]{1,0:T(8,128)(2,1)S(1)}, bf16[1280,512]{1,0:T(8,128)(2,1)}) fusion(bf16[1280,1,512]{2,1,0:T(2,128)(2,1)S(1)} %get-tuple-element.20, bf16[1280,1,512]{2,1,0:T(2,128)(2,1)S(1)} %get-tuple-element.19), kind=kLoop, calls=%fused_computation.2 | loop fusion | bytes 5242880 | tf_op jit(solution)/shard_map/squeeze | solution.py:560
  10.2 2.7 %constant_dynamic-slice_fusion = (bf16[1280,1,128]{2,1,0:T(2,128)(2,1)S(1)}, bf16[1280,1,128]{2,1,0:T(2,128)(2,1)S(1)}) fusion(bf16[1280,2,1280]{2,1,0:T(2,128)(2,1)} %param.11, s32[]{:T(128)S(6)} %select_n.35, s32[]{:T(128)S(6)} %add.35), kind=kLoop, calls=%fused_computation.19 | loop fusion | bytes 1310728 | tf_op jit(solution)/shard_map/slice | solution.py:560
  12.8 0.1 copy_bitcast_fusion.2
  12.9 0.8 dynamic_slice.11
  13.7 0.0 copy-start.4
  13.7 0.0 copy-start.3
  13.7 3.2 %multiply_convert_fusion.w = bf16[1280,1280]{1,0:T(8,128)(2,1)} fusion(bf16[1280,512]{1,0:T(8,128)(2,1)S(1)} %get-tuple-element.24, bf16[1280,512]{1,0:T(8,128)(2,1)} %get-tuple-element.25, bf16[1280,128]{1,0:T(8,128)(2,1)S(1)} %get-tuple-element.26, bf16[1280,128]{1,0:T(8,128)(2,1)S(1)} %get-tuple-element.27, f32[1280]{0:T(1024)S(1)} %dynamic_slice.11), kind=kLoop, calls=%fused_computation.1 | loop fusion | flops 16384000 | bytes 6558720 | tf_op jit(solution)/shard_map/convert_element_type | solution.py:562
  17.0 0.0 copy-done.4
  17.0 0.2 convert_reduce_fusion
  17.2 0.0 copy-done.3
  17.2 0.1 select_reduce_fusion
  17.3 0.0 copy-done
  17.3 0.6 gather_fusion
  17.9 0.1 convert_element_type.34
  18.0 0.1 broadcast_in_dim.49
  18.1 0.1 broadcast_in_dim.50
  18.2 0.0 copy-start.1
  18.2 0.0 copy-start.2
  18.2 115.3 %exchange.1 = (f32[4,512,256]{2,1,0:T(8,128)S(1)}, f32[2,512,256]{2,1,0:T(8,128)S(1)}, f32[4,8,128]{2,1,0:T(8,128)S(1)}) custom-call(bf16[4,2,64,1280]{3,2,1,0:T(8,128)(2,1)S(1)} %bitcast.11, f32[4,8,128]{2,1,0:T(8,128)S(1)} %broadcast_in_dim.51.lens, bf16[1280,1280]{1,0:T(8,128)(2,1)} %multiply_convert_fusion.w), custom_call_target="tpu_custom_call" | custom-call | flops 6710886400 | bytes 16777216 | tf_op jit(solution)/shard_map/exchange/pallas_call | solution.py:402
  133.5 0.3 fusion
  133.8 0.1 pad_maximum_fusion
  133.9 0.0 copy-done.1
  133.9 0.0 copy-done.2
  133.9 10.2 %attend.1 = (bf16[16,16,256]{2,1,0:T(8,128)(2,1)}, bf16[16,16,256]{2,1,0:T(8,128)(2,1)}, bf16[512,1024]{1,0:T(8,128)(2,1)S(1)}) custom-call(f32[4,512,256]{2,1,0:T(8,128)S(1)} %get-tuple-element.9.q_ref, f32[2,512,256]{2,1,0:T(8,128)S(1)} %get-tuple-element.10.kv_ref, f32[4,8,128]{2,1,0:T(8,128)S(1)} %get-tuple-element.11.len_ref, ...), custom_call_target="tpu_custom_call" | custom-call | tf_op jit(solution)/shard_map/attend/pallas_call | solution.py:509
  144.2 1.6 %reshape.44 = bf16[16,32,2,512]{3,2,1,0:T(2,128)(2,1)} reshape(bf16[512,1024]{1,0:T(8,128)(2,1)S(1)} %get-tuple-element.14) | data formatting | bytes 2097152 | tf_op jit(solution)/shard_map/reshape | solution.py:567
  (6 shorter events, 0.0 us)
Async XLA Ops:
  0.6 16.7 %copy-start = (bf16[16,32,1280]{2,1,0:T(8,128)(2,1)S(1)}, bf16[16,32,1280]{2,1,0:T(8,128)(2,1)}, u32[]{:S(2)}) copy-start(bf16[16,32,1280]{2,1,0:T(8,128)(2,1)} %param.7) | copy-start | bytes 3932164
  13.7 3.2 %copy-start.4 = (s32[16]{0:T(128)S(1)}, s32[16]{0:T(128)}, u32[]{:S(2)}) copy-start(s32[16]{0:T(128)} %param.9) | copy-start | bytes 196
  13.7 3.4 %copy-start.3 = (s32[16]{0:T(128)S(1)}, s32[16]{0:T(128)}, u32[]{:S(2)}) copy-start(s32[16]{0:T(128)} %param.8) | copy-start | bytes 196
  18.2 115.7 %copy-start.1 = (f32[128]{0:T(128)S(1)}, f32[128]{0:T(128)}, u32[]{:S(2)}) copy-start(f32[128]{0:T(128)} %param.12) | copy-start | bytes 1540
  18.2 115.7 %copy-start.2 = (f32[128]{0:T(128)S(1)}, f32[128]{0:T(128)}, u32[]{:S(2)}) copy-start(f32[128]{0:T(128)} %param.13) | copy-start | bytes 1540
